TPU v7x, 512 devices: a whole 4x8x8 slice. The times are simulated.
512 devices in a mesh: seq: 16 (over y, core), dp: 32 (over z, x).
Axes of the slice: x: 4, y: 8, z: 8, core: 2. Of those that a mesh axis runs over, the one named last changes fastest.
Arguments:
- queries: bfloat16 [32, 2048, 4096], P('dp', 'seq'), may hold values from -22 to 22
- key_vectors: bfloat16 [32, 2048, 512], P('dp', 'seq'), may hold values from -15 to 15
- value_vectors: bfloat16 [32, 2048, 512], P('dp', 'seq'), may hold values from -6 to 6
- forward_out: bfloat16 [32, 2048, 4096], P('dp', 'seq'), may hold values from -6 to 6
- out_grad: bfloat16 [32, 2048, 4096], P('dp', 'seq'), may hold values from -6 to 6
- segment_number: int32 [32, 2048], P('dp'), may hold values from 0 to 31, never falling along the last dimension, each value on 1 to 128 neighbouring positions
Outputs:
- query_grad: bfloat16 [32, 2048, 4096], P('dp', 'seq')
- key_grad: bfloat16 [32, 2048, 512], P('dp', 'seq')
- value_grad: bfloat16 [32, 2048, 512], P('dp', 'seq')
- bias_grad: float32 [5120], replicated
Inputs may be any that keep to these rules, and one draw needn't show every extreme that they name: `segment_number`: within each microbatch the rollout numbers never fall, all of 0 to 31 occur, each rollout holds 1 to 128 positions and one holds exactly 128.
All inputs are finite; a program needn't handle non-finite values.
Results may differ from a plain program's by a relative error of at most 0.0055.
Values may be sent and summed in bfloat16 or wider, within the bound.
No kernel may reach another device: no remote copies, remote signals or barrier semaphores. Data moves between devices by JAX's collectives and lax.ppermute only.
A program may use at most 64 MiB of HBM per device.

v0:
```python
import math

import jax
import jax.numpy as jnp
from jax import lax
from jax.sharding import PartitionSpec as P

HD = 128


def per_device(queries, key_vectors, value_vectors, forward_out, out_grad, segment_number):
    seq_ways = lax.axis_size("seq")
    tok_rows = queries.shape[1]
    seq_total = tok_rows * seq_ways
    shared_heads = key_vectors.shape[2] // HD
    copies = max(1, seq_ways // shared_heads)

    def widen(tensor):
        pieces = tensor.reshape(1, tok_rows, shared_heads, 1, HD)
        return jnp.broadcast_to(pieces, (1, tok_rows, shared_heads, copies, HD)).reshape(
            1, tok_rows, shared_heads * copies * HD
        )

    key_wide = widen(key_vectors)
    value_wide = widen(value_vectors)
    query_local, grad_local, output_local, key_local, value_local = (
        lax.all_to_all(queries, "seq", split_axis=2, concat_axis=1, tiled=True),
        lax.all_to_all(out_grad, "seq", split_axis=2, concat_axis=1, tiled=True),
        lax.all_to_all(forward_out, "seq", split_axis=2, concat_axis=1, tiled=True),
        lax.all_to_all(key_wide, "seq", split_axis=2, concat_axis=1, tiled=True),
        lax.all_to_all(value_wide, "seq", split_axis=2, concat_axis=1, tiled=True),
    )
    local_heads = query_local.shape[2] // HD
    products = grad_local.astype(jnp.float32) * output_local.astype(jnp.float32)
    delta_local = jnp.sum(products.reshape(seq_total, local_heads, HD), axis=2)
    local_shared = key_local.shape[2] // HD
    group_size = local_heads // local_shared
    query_heads = query_local.reshape(seq_total, local_shared, group_size, HD)
    grad_heads = grad_local.reshape(seq_total, local_shared, group_size, HD)
    key_heads = key_local.reshape(seq_total, local_shared, HD)
    value_heads = value_local.reshape(seq_total, local_shared, HD)
    delta_heads = delta_local.reshape(seq_total, local_shared, group_size)
    segment_row = segment_number[0]
    block_rows = min(max(8, 512 // local_heads), seq_total)
    score_scale = 1.0 / math.sqrt(HD)
    key_total = jnp.zeros((seq_total, local_shared, HD), jnp.float32)
    value_total = jnp.zeros((seq_total, local_shared, HD), jnp.float32)
    query_pieces = []
    for row_start in range(0, seq_total, block_rows):
        row_end = row_start + block_rows
        key_start = max(0, row_start - tok_rows)
        query_block = query_heads[row_start:row_end]
        grad_block = grad_heads[row_start:row_end]
        key_window = key_heads[key_start:row_end]
        value_window = value_heads[key_start:row_end]
        scores = (
            jnp.einsum(
                "igrd,jgd->grij", query_block, key_window, preferred_element_type=jnp.float32
            )
            * score_scale
        )
        key_positions = key_start + jnp.arange(row_end - key_start)
        row_positions = row_start + jnp.arange(block_rows)
        allowed = (segment_row[None, key_start:row_end] == segment_row[row_start:row_end, None]) & (
            key_positions[None, :] <= row_positions[:, None]
        )
        masked = jnp.where(allowed[None, None], scores, -jnp.inf)
        row_peak = jnp.max(masked, axis=3, keepdims=True)
        log_total = row_peak + jnp.log(jnp.sum(jnp.exp(masked - row_peak), axis=3, keepdims=True))
        weights = jnp.exp(masked - log_total)
        weights_low = weights.astype(jnp.bfloat16)
        value_total = value_total.at[key_start:row_end].add(
            jnp.einsum(
                "grij,igrd->jgd", weights_low, grad_block, preferred_element_type=jnp.float32
            )
        )
        weight_grad = jnp.einsum(
            "igrd,jgd->grij", grad_block, value_window, preferred_element_type=jnp.float32
        )
        delta_block = jnp.transpose(delta_heads[row_start:row_end], (1, 2, 0))[..., None]
        score_low = (weights * (weight_grad - delta_block)).astype(jnp.bfloat16)
        query_pieces.append(
            (
                jnp.einsum(
                    "grij,jgd->igrd", score_low, key_window, preferred_element_type=jnp.float32
                )
                * score_scale
            ).astype(jnp.bfloat16)
        )
        key_total = key_total.at[key_start:row_end].add(
            jnp.einsum("grij,igrd->jgd", score_low, query_block, preferred_element_type=jnp.float32)
        )
    query_head_grad = jnp.concatenate(query_pieces, axis=0).reshape(1, seq_total, local_heads * HD)
    key_part = (key_total * score_scale).reshape(1, seq_total, local_shared * HD)
    value_part = value_total.reshape(1, seq_total, local_shared * HD)
    query_grad = lax.all_to_all(query_head_grad, "seq", split_axis=1, concat_axis=2, tiled=True)
    key_back, value_back = (
        lax.all_to_all(key_part, "seq", split_axis=1, concat_axis=2, tiled=True),
        lax.all_to_all(value_part, "seq", split_axis=1, concat_axis=2, tiled=True),
    )
    key_grad = (
        jnp.sum(key_back.reshape(1, tok_rows, shared_heads, copies, HD), axis=3)
        .reshape(1, tok_rows, shared_heads * HD)
        .astype(jnp.bfloat16)
    )
    value_grad = (
        jnp.sum(value_back.reshape(1, tok_rows, shared_heads, copies, HD), axis=3)
        .reshape(1, tok_rows, shared_heads * HD)
        .astype(jnp.bfloat16)
    )
    column_sums = jnp.concatenate(
        [
            jnp.sum(query_grad.astype(jnp.float32), axis=(0, 1)),
            jnp.sum(key_grad.astype(jnp.float32), axis=(0, 1)),
            jnp.sum(value_grad.astype(jnp.float32), axis=(0, 1)),
        ]
    )
    bias_grad = lax.psum(column_sums, ("seq", "dp"))
    return (query_grad, key_grad, value_grad, bias_grad)


def solution(mesh):
    in_specs = (
        P("dp", "seq", None),
        P("dp", "seq", None),
        P("dp", "seq", None),
        P("dp", "seq", None),
        P("dp", "seq", None),
        P("dp", None),
    )
    out_specs = (P("dp", "seq", None), P("dp", "seq", None), P("dp", "seq", None), P())
    return jax.shard_map(
        per_device, mesh=mesh, in_specs=in_specs, out_specs=out_specs, check_vma=False
    )
```

profile of v0, /device:TPU:1, one launch (start us, length us, event | category | flops | bytes accessed | tf_op | source)
XLA Modules:
  0.0 478.9 jit_solution(2034112857784955749)
XLA Ops:
  0.6 1.0 copy.317
  1.8 8.1 %copy.408 = bf16[1,128,2048]{1,0,2:T(2,128)(2,1)S(1)} copy(bf16[1,128,2048]{1,2,0:T(8,128)(2,1)S(1)} %bitcast.706) | data formatting | bytes 1048576 | tf_op jit(solution)/shard_map/broadcast_in_dim | solution.py:20
  10.4 11.4 %reduce.70 = bf16[2048,128]{1,0:T(8,128)(2,1)S(1)} reduce(bf16[2048,1,128]{2,1,0:T(2,128)(2,1)S(1)} %bitcast.700, bf16[]{:T(256)} %broadcast.688), dimensions={1}, to_apply=%bitcast.679.reduce_sub_computation | reduce | bytes 1048578
  22.7 10.5 %all-to-all-start = ((bf16[16,2,8192]{2,1,0:T(2,128)(2,1)}), bf16[16,2,8192]{2,1,0:T(2,128)(2,1)S(1)}, u32[]{:S(2)}, u32[]{:S(2)}) async-start(bf16[16,2,8192]{2,1,0:T(2,128)(2,1)} %reshape.1821), calls=%async_computation | async-start | bytes 1048576 | tf_op jit(solution)/shard_map/all_to_all | solution.py:30
  33.5 8.1 %copy.407 = bf16[1,128,2048]{1,0,2:T(2,128)(2,1)S(1)} copy(bf16[1,128,2048]{1,2,0:T(8,128)(2,1)S(1)} %bitcast.707) | data formatting | bytes 1048576 | tf_op jit(solution)/shard_map/broadcast_in_dim | solution.py:20
  41.7 11.5 %reduce.69 = bf16[2048,128]{1,0:T(8,128)(2,1)S(1)} reduce(bf16[2048,1,128]{2,1,0:T(2,128)(2,1)S(1)} %bitcast.701, bf16[]{:T(256)} %broadcast.688), dimensions={1}, to_apply=%bitcast.678.reduce_sub_computation | reduce | bytes 1048578
  54.9 7.8 %all-to-all-start.2 = ((bf16[16,2,8192]{2,1,0:T(2,128)(2,1)}), bf16[16,2,8192]{2,1,0:T(2,128)(2,1)}, u32[]{:S(2)}, u32[]{:S(2)}) async-start(bf16[16,2,8192]{2,1,0:T(2,128)(2,1)} %reshape.1819), calls=%async_computation.2 | async-start | bytes 1048576 | tf_op jit(solution)/shard_map/all_to_all | solution.py:31
  62.8 2.8 copy.222
  65.6 22.3 %reduce.71 = bf16[4096,128]{1,0:T(8,128)(2,1)S(1)} reduce(bf16[4096,1,128]{2,1,0:T(2,128)(2,1)S(1)} %bitcast.690, bf16[]{:T(256)} %broadcast.688), dimensions={1}, to_apply=%bitcast.627.reduce_sub_computation | reduce | bytes 2097154
  87.9 1.1 reshape.1823
  89.0 7.2 %all-to-all-start.1 = ((bf16[16,2,16384]{2,1,0:T(2,128)(2,1)}), bf16[16,2,16384]{2,1,0:T(2,128)(2,1)S(1)}, u32[]{:S(2)}, u32[]{:S(2)}) async-start(bf16[16,2,16384]{2,1,0:T(2,128)(2,1)} %reshape.1823), calls=%async_computation.1 | async-start | bytes 2097152 | tf_op jit(solution)/shard_map/all_to_all | solution.py:27
  96.2 5.0 %copy.231 = bf16[1,128,4096]{1,0,2:T(2,128)(2,1)S(1)} copy(bf16[1,128,4096]{2,1,0:T(8,128)(2,1)} %param.41) | data formatting | bytes 2097152 | tf_op args[3]
  101.3 23.3 %reduce.72 = bf16[4096,128]{1,0:T(8,128)(2,1)} reduce(bf16[4096,1,128]{2,1,0:T(2,128)(2,1)S(1)} %bitcast.691, bf16[]{:T(256)} %broadcast.688), dimensions={1}, to_apply=%bitcast.629.reduce_sub_computation | reduce | bytes 2097154
  124.5 2.1 reshape.1825
  126.7 7.6 %all-to-all-start.4 = ((bf16[16,2,16384]{2,1,0:T(2,128)(2,1)}), bf16[16,2,16384]{2,1,0:T(2,128)(2,1)}, u32[]{:S(2)}, u32[]{:S(2)}) async-start(bf16[16,2,16384]{2,1,0:T(2,128)(2,1)} %reshape.1825), calls=%async_computation.4 | async-start | bytes 2097152 | tf_op jit(solution)/shard_map/all_to_all | solution.py:29
  134.3 5.0 %copy.228 = bf16[1,128,4096]{1,0,2:T(2,128)(2,1)S(1)} copy(bf16[1,128,4096]{2,1,0:T(8,128)(2,1)} %param.42) | data formatting | bytes 2097152 | tf_op args[4]
  139.4 23.3 %reduce.73 = bf16[4096,128]{1,0:T(8,128)(2,1)} reduce(bf16[4096,1,128]{2,1,0:T(2,128)(2,1)S(1)} %bitcast.692, bf16[]{:T(256)} %broadcast.688), dimensions={1}, to_apply=%bitcast.631.reduce_sub_computation | reduce | bytes 2097154
  162.6 2.2 reshape.1827
  165.8 1.0 compare_and_fusion
  168.6 7.2 %all-to-all-start.3 = ((bf16[16,2,16384]{2,1,0:T(2,128)(2,1)}), bf16[16,2,16384]{2,1,0:T(2,128)(2,1)}, u32[]{:S(2)}, u32[]{:S(2)}) async-start(bf16[16,2,16384]{2,1,0:T(2,128)(2,1)} %reshape.1827), calls=%async_computation.3 | async-start | bytes 2097152 | tf_op jit(solution)/shard_map/all_to_all | solution.py:28
  183.3 2.2 reshape.1820
  191.7 1.0 reshape.1824
  193.8 4.4 reshape.1826
  198.2 1.1 fusion.171
  199.4 3.2 bitcast_convert_fusion
  202.7 1.2 all-to-all-done.3
  203.9 4.3 reshape.1828
  210.3 1.2 copy.232
  211.6 1.7 mul.171
  213.3 1.8 reduce_sum.133
  227.2 1.7 copy.273
  228.9 1.6 reshape.1742
  230.5 1.7 copy.266
  232.1 1.6 reshape.1737
  233.7 1.7 copy.259
  235.4 1.6 reshape.1732
  237.8 1.6 reshape.1727
  241.0 1.3 fusion.39
  242.3 2.0 fusion.98
  244.4 1.0 fusion.40
  245.5 1.0 fusion.96
  248.8 1.0 fusion.92
  250.2 1.0 fusion.90
  251.5 1.0 fusion.88
  253.6 1.0 fusion.86
  254.5 2.3 copy.283
  256.8 4.6 copy.284
  261.4 11.5 %reduce.74 = bf16[2048,256]{1,0:T(8,128)(2,1)} reduce(bf16[2048,1,256]{2,1,0:T(2,128)(2,1)S(1)} %bitcast.689, bf16[]{:T(256)} %broadcast.688), dimensions={1}, to_apply=%bitcast.633.reduce_sub_computation | reduce | bytes 2097154
  272.9 2.2 reshape.1829
  275.1 6.5 %all-to-all-start.5 = ((bf16[16,2,16384]{2,1,0:T(2,128)(2,1)}), bf16[16,2,16384]{2,1,0:T(2,128)(2,1)S(1)}, u32[]{:S(2)}, u32[]{:S(2)}) async-start(bf16[16,2,16384]{2,1,0:T(2,128)(2,1)} %reshape.1829), calls=%async_computation.5 | async-start | bytes 2097152 | tf_op jit(solution)/shard_map/all_to_all | solution.py:96
  281.7 1.4 fusion.84
  285.0 1.1 broadcast_multiply_fusion
  286.0 23.4 %all-to-all-done.5 = bf16[16,2,16384]{2,1,0:T(2,128)(2,1)S(1)} async-done(((bf16[16,2,16384]{2,1,0:T(2,128)(2,1)}), bf16[16,2,16384]{2,1,0:T(2,128)(2,1)S(1)}, u32[]{:S(2)}, u32[]{:S(2)}) %all-to-all-start.5) | async-done | bytes 1048608 | tf_op jit(solution)/shard_map/all_to_all | solution.py:96
  309.4 3.6 all-to-all-start.6
  313.3 1.4 fusion.70
  316.6 1.0 copy.429
  318.5 22.3 %all-to-all-done.6 = f32[1,2048,128]{2,0,1:T(1,128)S(1)} async-done(((f32[1,2048,128]{2,0,1:T(1,128)}), f32[1,2048,128]{2,0,1:T(1,128)S(1)}, u32[]{:S(2)}, u32[]{:S(2)}) %all-to-all-start.6) | async-done | bytes 1048608 | tf_op jit(solution)/shard_map/all_to_all | solution.py:98
  340.8 1.0 copy-done.17
  341.8 4.2 all-to-all-start.7
  346.1 1.1 reshape.1830
  348.9 24.4 %all-to-all-done.7 = f32[1,2048,128]{2,0,1:T(1,128)} async-done(((f32[1,2048,128]{2,0,1:T(1,128)}), f32[1,2048,128]{2,0,1:T(1,128)}, u32[]{:S(2)}, u32[]{:S(2)}) %all-to-all-start.7) | async-done | bytes 1048608 | tf_op jit(solution)/shard_map/all_to_all | solution.py:99
  373.4 1.3 reduce_sum.142
  374.8 1.3 copy.306
  377.7 100.8 %psum.7 = f32[5120]{0:T(1024)} all-reduce(f32[5120]{0:T(1024)S(1)} %pad_maximum_fusion), channel_id=1, replica_groups=mesh['seq'=16,'dp'=32] {'seq','dp'}, use_global_device_ids=true, to_apply=%region_22.23 | all-reduce | flops 5120 | bytes 40960 | tf_op jit(solution)/shard_map/psum | solution.py:118
  (364 shorter events, 49.3 us)
Async XLA Ops:
  9.9 23.4 %copy-start.88 = (bf16[1,128,512]{2,1,0:T(8,128)(2,1)S(1)}, bf16[1,128,512]{2,1,0:T(8,128)(2,1)}, u32[]{:S(2)}) copy-start(bf16[1,128,512]{2,1,0:T(8,128)(2,1)} %param.40) | copy-start | bytes 393220
  22.7 31.4 %all-to-all-start = ((bf16[16,2,8192]{2,1,0:T(2,128)(2,1)}), bf16[16,2,8192]{2,1,0:T(2,128)(2,1)S(1)}, u32[]{:S(2)}, u32[]{:S(2)}) async-start(bf16[16,2,8192]{2,1,0:T(2,128)(2,1)} %reshape.1821), calls=%async_computation | async-start | bytes 1048576 | tf_op jit(solution)/shard_map/all_to_all | solution.py:30
  41.7 21.1 %copy-start.47 = (bf16[1,128,4096]{2,1,0:T(8,128)(2,1)S(1)}, bf16[1,128,4096]{2,1,0:T(8,128)(2,1)}, u32[]{:S(2)}) copy-start(bf16[1,128,4096]{2,1,0:T(8,128)(2,1)} %param.38) | copy-start | bytes 3145732
  54.9 34.1 %all-to-all-start.2 = ((bf16[16,2,8192]{2,1,0:T(2,128)(2,1)}), bf16[16,2,8192]{2,1,0:T(2,128)(2,1)}, u32[]{:S(2)}, u32[]{:S(2)}) async-start(bf16[16,2,8192]{2,1,0:T(2,128)(2,1)} %reshape.1819), calls=%async_computation.2 | async-start | bytes 1048576 | tf_op jit(solution)/shard_map/all_to_all | solution.py:31
  89.0 37.7 %all-to-all-start.1 = ((bf16[16,2,16384]{2,1,0:T(2,128)(2,1)}), bf16[16,2,16384]{2,1,0:T(2,128)(2,1)S(1)}, u32[]{:S(2)}, u32[]{:S(2)}) async-start(bf16[16,2,16384]{2,1,0:T(2,128)(2,1)} %reshape.1823), calls=%async_computation.1 | async-start | bytes 2097152 | tf_op jit(solution)/shard_map/all_to_all | solution.py:27
  126.7 41.9 %all-to-all-start.4 = ((bf16[16,2,16384]{2,1,0:T(2,128)(2,1)}), bf16[16,2,16384]{2,1,0:T(2,128)(2,1)}, u32[]{:S(2)}, u32[]{:S(2)}) async-start(bf16[16,2,16384]{2,1,0:T(2,128)(2,1)} %reshape.1825), calls=%async_computation.4 | async-start | bytes 2097152 | tf_op jit(solution)/shard_map/all_to_all | solution.py:29
  139.4 25.5 %copy-start.97 = (s32[1,2048]{1,0:T(1,128)S(1)}, s32[1,2048]{1,0:T(1,128)}, u32[]{:S(2)}) copy-start(s32[1,2048]{1,0:T(1,128)} %param.43) | copy-start | bytes 24580
  162.6 13.9 %copy-start.33 = (bf16[16,2,8192]{2,1,0:T(2,128)(2,1)S(1)}, bf16[16,2,8192]{2,1,0:T(2,128)(2,1)}, u32[]{:S(2)}) copy-start(bf16[16,2,8192]{2,1,0:T(2,128)(2,1)} %copy-done.32) | copy-start | bytes 1572868
  168.6 35.3 %all-to-all-start.3 = ((bf16[16,2,16384]{2,1,0:T(2,128)(2,1)}), bf16[16,2,16384]{2,1,0:T(2,128)(2,1)}, u32[]{:S(2)}, u32[]{:S(2)}) async-start(bf16[16,2,16384]{2,1,0:T(2,128)(2,1)} %reshape.1827), calls=%async_computation.3 | async-start | bytes 2097152 | tf_op jit(solution)/shard_map/all_to_all | solution.py:28
  193.8 5.6 %copy-start.66 = (bf16[256,2,128]{2,1,0:T(2,128)(2,1)}, bf16[256,2,128]{2,1,0:T(2,128)(2,1)S(1)}, u32[]{:S(2)}) copy-start(bf16[256,2,128]{2,1,0:T(2,128)(2,1)S(1)} %reshape.1710) | copy-start | bytes 393220
  213.3 2.8 copy-start.67
  213.3 3.7 copy-start.96
  213.3 4.6 copy-start.64
  217.0 2.8 copy-start.80
  217.0 2.8 copy-start.93
  218.1 6.2 %copy-start.48 = (bf16[256,2,128]{2,1,0:T(2,128)(2,1)}, bf16[256,2,128]{2,1,0:T(2,128)(2,1)S(1)}, u32[]{:S(2)}) copy-start(bf16[256,2,128]{2,1,0:T(2,128)(2,1)S(1)} %reshape.1745) | copy-start | bytes 393220
  218.3 5.0 %copy-start.50 = (bf16[256,2,128]{2,1,0:T(2,128)(2,1)}, bf16[256,2,128]{2,1,0:T(2,128)(2,1)S(1)}, u32[]{:S(2)}) copy-start(bf16[256,2,128]{2,1,0:T(2,128)(2,1)S(1)} %reshape.1740) | copy-start | bytes 393220
  218.5 3.8 copy-start.52
  218.6 2.7 copy-start.54
  220.6 23.8 %copy-start.1 = (f32[1,2,256,384]{2,3,1,0:T(8,128)}, f32[1,2,256,384]{2,3,1,0:T(8,128)S(1)}, u32[]{:S(2)}) copy-start(f32[1,2,256,384]{2,3,1,0:T(8,128)S(1)} %get-tuple-element.266) | copy-start | bytes 2359300
  221.1 25.3 %copy-start.3 = (f32[1,2,256,384]{2,3,1,0:T(8,128)}, f32[1,2,256,384]{2,3,1,0:T(8,128)S(1)}, u32[]{:S(2)}) copy-start(f32[1,2,256,384]{2,3,1,0:T(8,128)S(1)} %get-tuple-element.268) | copy-start | bytes 2359300
  222.7 2.8 copy-start.63
  223.7 13.3 %copy-start.62 = (bf16[1,2,128,256]{2,3,1,0:T(8,128)(2,1)S(1)}, bf16[1,2,128,256]{2,3,1,0:T(8,128)(2,1)}, u32[]{:S(2)}) copy-start(bf16[1,2,128,256]{2,3,1,0:T(8,128)(2,1)} %get-tuple-element.219) | copy-start | bytes 393220
  224.3 15.1 %copy-start.61 = (bf16[1,2,128,256]{2,3,1,0:T(8,128)(2,1)S(1)}, bf16[1,2,128,256]{2,3,1,0:T(8,128)(2,1)}, u32[]{:S(2)}) copy-start(bf16[1,2,128,256]{2,3,1,0:T(8,128)(2,1)} %get-tuple-element.220) | copy-start | bytes 393220
  224.6 15.6 %copy-start.60 = (bf16[1,2,128,256]{2,3,1,0:T(8,128)(2,1)S(1)}, bf16[1,2,128,256]{2,3,1,0:T(8,128)(2,1)}, u32[]{:S(2)}) copy-start(bf16[1,2,128,256]{2,3,1,0:T(8,128)(2,1)} %get-tuple-element.221) | copy-start | bytes 393220
  227.2 25.3 %copy-start.35 = (bf16[256,2,128]{2,1,0:T(2,128)(2,1)}, bf16[256,2,128]{2,1,0:T(2,128)(2,1)S(1)}, u32[]{:S(2)}) copy-start(bf16[256,2,128]{2,1,0:T(2,128)(2,1)S(1)} %reshape.1747) | copy-start | bytes 393220
  241.0 3.4 copy-start.45
  241.0 3.4 copy-start.86
  241.0 4.4 copy-start.79
  241.0 5.5 %copy-start.43 = (bf16[256,2,128]{2,1,0:T(2,128)(2,1)S(1)}, bf16[256,2,128]{2,1,0:T(2,128)(2,1)}, u32[]{:S(2)}) copy-start(bf16[256,2,128]{2,1,0:T(2,128)(2,1)} %reshape.1727) | copy-start | bytes 393220
  241.0 5.5 %copy-start.85 = (bf16[1,3,128,128]{3,2,1,0:T(8,128)(2,1)S(1)}, bf16[1,3,128,128]{3,2,1,0:T(8,128)(2,1)}, u32[]{:S(2)}) copy-start(bf16[1,3,128,128]{3,2,1,0:T(8,128)(2,1)} %copy.251) | copy-start | bytes 294916
  241.0 5.5 %copy-start.110 = (f32[2,256]{1,0:T(2,128)S(1)}, f32[2,256]{1,0:T(2,128)}, u32[]{:S(2)}) copy-start(f32[2,256]{1,0:T(2,128)} %get-tuple-element.249) | copy-start | bytes 6148
  242.3 5.2 %copy-start.77 = (bf16[1,3,128,128]{3,2,1,0:T(8,128)(2,1)S(1)}, bf16[1,3,128,128]{3,2,1,0:T(8,128)(2,1)}, u32[]{:S(2)}) copy-start(bf16[1,3,128,128]{3,2,1,0:T(8,128)(2,1)} %copy.248) | copy-start | bytes 294916
  244.3 4.1 copy-start.6
  244.3 4.1 copy-start.41
  244.4 4.2 copy-start.84
  244.4 4.2 copy-start.98
  244.4 4.2 copy-start.109
  245.4 4.4 copy-start.19
  245.4 3.4 copy-start.75
  246.4 3.4 copy-start.9
  246.4 3.4 copy-start.39
  246.4 3.4 copy-start.83
  246.4 3.4 copy-start.100
  246.4 3.4 copy-start.108
  247.5 2.7 copy-start.73
  248.5 2.7 copy-start.12
  248.5 2.7 copy-start.37
  248.5 2.7 copy-start.82
  248.5 2.7 copy-start.102
  248.5 2.7 copy-start.107
  248.8 3.6 copy-start.23
  248.8 2.6 copy-start.71
  249.8 2.7 copy-start.15
  249.8 2.7 copy-start.81
  249.8 2.7 copy-start.104
  249.8 2.7 copy-start.106
  250.2 3.4 copy-start.69
  272.9 8.7 %copy-start.34 = (f32[256,1,128]{2,0,1:T(8,128)S(1)}, f32[256,1,128]{2,0,1:T(8,128)}, u32[]{:S(2)}) copy-start(f32[256,1,128]{2,0,1:T(8,128)} %convolution_bitcast_fusion.23) | copy-start | bytes 393220
  275.0 8.1 %copy-start.20 = (bf16[2,256,384]{1,2,0:T(8,128)(2,1)S(1)}, bf16[2,256,384]{1,2,0:T(8,128)(2,1)}, u32[]{:S(2)}) copy-start(bf16[2,256,384]{1,2,0:T(8,128)(2,1)} %copy-done.19) | copy-start | bytes 1179652
  275.1 8.4 %copy-start.22 = (bf16[2,256,384]{1,2,0:T(8,128)(2,1)S(1)}, bf16[2,256,384]{1,2,0:T(8,128)(2,1)}, u32[]{:S(2)}) copy-start(bf16[2,256,384]{1,2,0:T(8,128)(2,1)} %copy-done.21) | copy-start | bytes 1179652
  275.1 34.3 %all-to-all-start.5 = ((bf16[16,2,16384]{2,1,0:T(2,128)(2,1)}), bf16[16,2,16384]{2,1,0:T(2,128)(2,1)S(1)}, u32[]{:S(2)}, u32[]{:S(2)}) async-start(bf16[16,2,16384]{2,1,0:T(2,128)(2,1)} %reshape.1829), calls=%async_computation.5 | async-start | bytes 2097152 | tf_op jit(solution)/shard_map/all_to_all | solution.py:96
  309.4 31.5 %all-to-all-start.6 = ((f32[1,2048,128]{2,0,1:T(1,128)}), f32[1,2048,128]{2,0,1:T(1,128)S(1)}, u32[]{:S(2)}, u32[]{:S(2)}) async-start(f32[1,2048,128]{2,0,1:T(1,128)} %bitcast.698), calls=%async_computation.6 | async-start | bytes 2097152 | tf_op jit(solution)/shard_map/all_to_all | solution.py:98
  341.8 31.6 %all-to-all-start.7 = ((f32[1,2048,128]{2,0,1:T(1,128)}), f32[1,2048,128]{2,0,1:T(1,128)}, u32[]{:S(2)}, u32[]{:S(2)}) async-start(f32[1,2048,128]{2,0,1:T(1,128)} %bitcast.221), calls=%async_computation.7 | async-start | bytes 2097152 | tf_op jit(solution)/shard_map/all_to_all | solution.py:99
  (55 other events, 91.8 us)
where the time goes:
time: 488 us; the launch traced here: 479 us
  other arithmetic  119 us (24%)
  local copies, waits for them, and re-layouts  107 us (22%)
  blocking collectives  101 us (21%)
  waiting for transfers between devices  71.3 us (15%)
  starting transfers between devices  54.7 us (11%)
  matrix products  23.5 us (5%)
    unnamed x6, other arithmetic  103 us
    psum x1, blocking collectives, per_device(): bias_grad = lax.psum(column_sums, ('seq', 'dp'))  101 us
    unnamed x248, local copies, waits for them, and re-layouts  46.4 us
    all_to_all x1, waiting for transfers between devices, per_device(): lax.all_to_all(value_part, 'seq', split_axis=1, concat_axis=2, tiled=True)  24.4 us
    all_to_all x1, waiting for transfers between devices, per_device(): lax.all_to_all(query_head_grad, 'seq', split_axis=1, concat_axis=2, tiled...  23.4 us
    all_to_all x1, waiting for transfers between devices, per_device(): lax.all_to_all(key_part, 'seq', split_axis=1, concat_axis=2, tiled=True)  22.3 us
    broadcast_in_dim x6, local copies, waits for them, and re-layouts, widen(): jnp.broadcast_to(pieces, (1, tok_rows, shared_heads, copies, HD))  17.6 us
    all_to_all x1, starting transfers between devices, per_device(): lax.all_to_all(key_wide, 'seq', split_axis=2, concat_axis=1, tiled=True)  10.5 us
  transfers between devices with their start and end apart: 8, of which 4 were waited for; matrix products, arithmetic and copies ran while one was open for 31% of the time, Pallas kernels for 0%

commit v1 on v0

v1 whole, which is shorter than its diff:
```python
import functools
import math

import jax
import jax.numpy as jnp
from jax import lax
from jax.experimental import pallas as pl
from jax.experimental.pallas import tpu as pltpu
from jax.sharding import PartitionSpec as P

HD = 128
ROWS = 128
GROUP = 8
NEG = -1e30
SCALE = 1.0 / math.sqrt(HD)
SCALE2 = SCALE * math.log2(math.e)
TN = (((1,), (1,)), ((), ()))
NN = (((1,), (0,)), ((), ()))


def dot(a, b, dims=NN):
    return lax.dot_general(a, b, dims, preferred_element_type=jnp.float32)


def attention_kernel(
    me_ref, seg_ref, q_ref, o_ref, do_ref, kc_ref, vc_ref, kp_ref, vp_ref,
    dq_ref, own_ref, back_ref, sums_ref,
    mask_ref, w_ref, ds_ref,
):
    group = pl.program_id(0)
    shared = pl.num_programs(0)

    @pl.when(group == 0)
    def _():
        me = me_ref[0]
        before = jnp.maximum(me - 1, 0)
        seg_own = jnp.broadcast_to(seg_ref[pl.ds(me, 1), :], (ROWS, ROWS))
        seg_before = jnp.broadcast_to(seg_ref[pl.ds(before, 1), :], (ROWS, ROWS))
        key = lax.broadcasted_iota(jnp.int32, (ROWS, ROWS), 0)
        row = lax.broadcasted_iota(jnp.int32, (ROWS, ROWS), 1)
        own_col = jnp.sum(jnp.where(key == row, seg_own, 0), axis=1, keepdims=True)
        before_col = jnp.sum(jnp.where(key == row, seg_before, 0), axis=1, keepdims=True)
        mask_ref[0:ROWS, :] = jnp.where((before_col == seg_own) & (me > 0), 0.0, NEG)
        mask_ref[ROWS : 2 * ROWS, :] = jnp.where((own_col == seg_own) & (key <= row), 0.0, NEG)

    keys = jnp.concatenate([kp_ref[...], kc_ref[...]], axis=0)
    values = jnp.concatenate([vp_ref[...], vc_ref[...]], axis=0)
    keys_t = keys.T
    mask = mask_ref[...]
    query_sums = []
    for head in range(GROUP):
        at = slice(head * HD, (head + 1) * HD)
        q = q_ref[:, at]
        do = do_ref[:, at]
        products = do.astype(jnp.float32) * o_ref[:, at].astype(jnp.float32)
        delta = jnp.sum(products.T, axis=0, keepdims=True)
        scores = dot(keys, q, TN) * SCALE2 + mask
        peak = jnp.max(scores, axis=0, keepdims=True)
        powers = jnp.exp2(scores - peak)
        total = jnp.sum(powers, axis=0, keepdims=True)
        weights = powers * (1.0 / total)
        w_ref[:, at] = weights.astype(jnp.bfloat16)
        score_grad = weights * (dot(values, do, TN) - delta)
        score_low = score_grad.astype(jnp.bfloat16)
        ds_ref[:, at] = score_low
        dq = (dot(keys_t, score_low).T * SCALE).astype(jnp.bfloat16)
        dq_ref[:, at] = dq
        query_sums.append(jnp.sum(dq.astype(jnp.float32), axis=0, keepdims=True))
    sums_ref[pl.ds(group * GROUP, GROUP), :] = jnp.concatenate(query_sums, axis=0)

    def stacked(ref):
        return jnp.concatenate([ref[:, h * HD : (h + 1) * HD] for h in range(GROUP)], axis=0)

    key_part = dot(ds_ref[...], stacked(q_ref)) * SCALE
    value_part = dot(w_ref[...], stacked(do_ref))
    back_ref[0] = key_part[:ROWS]
    back_ref[1] = value_part[:ROWS]
    own_ref[0] = key_part[ROWS:]
    own_ref[1] = value_part[ROWS:]
    base = shared * GROUP
    sums_ref[pl.ds(base + group, 1), :] = jnp.sum(key_part, axis=0, keepdims=True)
    sums_ref[pl.ds(base + shared + group, 1), :] = jnp.sum(value_part, axis=0, keepdims=True)


def attention(me, segments, queries, forward_out, out_grad, own, before):
    shared = own.shape[1] // (2 * HD)
    wide = pl.BlockSpec((ROWS, GROUP * HD), lambda g: (0, g))
    key_spec = pl.BlockSpec((ROWS, HD), lambda g: (0, g))
    value_spec = pl.BlockSpec((ROWS, HD), lambda g: (0, shared + g))
    part_spec = pl.BlockSpec((2, ROWS, HD), lambda g: (0, 0, g))
    sum_rows = shared * GROUP + 2 * shared
    return pl.pallas_call(
        attention_kernel,
        grid=(shared,),
        in_specs=[
            pl.BlockSpec(memory_space=pltpu.SMEM),
            pl.BlockSpec(segments.shape, lambda g: (0, 0)),
            wide, wide, wide,
            key_spec, value_spec, key_spec, value_spec,
        ],
        out_specs=[wide, part_spec, part_spec, pl.BlockSpec((sum_rows, HD), lambda g: (0, 0))],
        out_shape=[
            jax.ShapeDtypeStruct(queries.shape, jnp.bfloat16),
            jax.ShapeDtypeStruct((2, ROWS, shared * HD), jnp.float32),
            jax.ShapeDtypeStruct((2, ROWS, shared * HD), jnp.float32),
            jax.ShapeDtypeStruct((sum_rows, HD), jnp.float32),
        ],
        scratch_shapes=[
            pltpu.VMEM((2 * ROWS, ROWS), jnp.float32),
            pltpu.VMEM((2 * ROWS, GROUP * HD), jnp.bfloat16),
            pltpu.VMEM((2 * ROWS, GROUP * HD), jnp.bfloat16),
        ],
        compiler_params=pltpu.CompilerParams(vmem_limit_bytes=32 * 1024 * 1024),
        cost_estimate=pl.CostEstimate(
            flops=10 * 2 * ROWS * ROWS * HD * shared * GROUP,
            bytes_accessed=5 * 1024 * 1024,
            transcendentals=2 * ROWS * ROWS * shared * GROUP,
        ),
    )(me, segments, queries, forward_out, out_grad, own, own, before, before)


def cosets(size, masks):
    span = [0]
    for m in masks:
        span = span + [a ^ m for a in span]
    groups, seen = [], set()
    for i in range(size):
        if i not in seen:
            group = sorted(i ^ a for a in span)
            groups.append(group)
            seen |= set(group)
    return groups


def group_sum(x, axis, masks):
    groups = cosets(lax.axis_size(axis), masks)
    count = len(groups[0])
    if count == 2:
        parts = lax.all_gather(x, axis, axis_index_groups=groups)
    else:
        copies = jnp.broadcast_to(x[None], (count,) + x.shape)
        parts = lax.all_to_all(
            copies, axis, split_axis=0, concat_axis=0, tiled=True, axis_index_groups=groups
        )
    return jnp.sum(parts, axis=0)


def global_sum(x):
    for axis, masks in (("seq", [1]), ("seq", [2, 4, 8]), ("dp", [1, 2]), ("dp", [4, 8, 16])):
        x = group_sum(x, axis, [m for m in masks if m < lax.axis_size(axis)])
    return x


def per_device(queries, key_vectors, value_vectors, forward_out, out_grad, segment_number):
    ways = lax.axis_size("seq")
    me = lax.axis_index("seq")
    own = jnp.concatenate([key_vectors[0], value_vectors[0]], axis=1)
    before = lax.ppermute(own, "seq", [(i, i + 1) for i in range(ways - 1)])
    segments = segment_number.reshape(ways, ROWS)
    query_grad, kept, back, sums = attention(
        me.astype(jnp.int32).reshape(1), segments, queries[0], forward_out[0], out_grad[0], own, before
    )
    returned = lax.ppermute(back, "seq", [(i + 1, i) for i in range(ways - 1)])
    both = (kept + returned).astype(jnp.bfloat16)
    bias_grad = global_sum(sums).reshape(-1)
    return (query_grad[None], both[0][None], both[1][None], bias_grad)


def solution(mesh):
    rows = P("dp", "seq", None)
    return jax.shard_map(
        per_device,
        mesh=mesh,
        in_specs=(rows, rows, rows, rows, rows, P("dp", None)),
        out_specs=(rows, rows, rows, P()),
        check_vma=False,
    )
```

time: 488 us -> 75.4 us (0.15)
  the two profiles are of different devices: /device:TPU:1 before, /device:TPU:2 now
where the time goes in v1:
time: 75.4 us; the launch traced here: 75 us
  blocking collectives  34.7 us (46%)
  starting transfers between devices  13.3 us (18%)
  waiting for transfers between devices  9.72 us (13%)
  Pallas kernels  9.69 us (13%)
  local copies, waits for them, and re-layouts  5.08 us (7%)
  other arithmetic  1.73 us (2%)
    all_to_all x2, blocking collectives, group_sum(): lax.all_to_all(copies, axis, split_axis=0, concat_axis=0, tiled=True, axi...  28.6 us
    all_to_all x1, starting transfers between devices, group_sum(): lax.all_to_all(copies, axis, split_axis=0, concat_axis=0, tiled=True, axi...  10.3 us
    pallas_call x1, Pallas kernels, attention(): pl.pallas_call(attention_kernel, grid=(shared,), in_specs=[pl.BlockSpec(m...  9.69 us
    all_to_all x1, waiting for transfers between devices, group_sum(): lax.all_to_all(copies, axis, split_axis=0, concat_axis=0, tiled=True, axi...  8.61 us
    all_gather x1, blocking collectives, group_sum(): parts = lax.all_gather(x, axis, axis_index_groups=groups)  6.13 us
    unnamed x8, local copies, waits for them, and re-layouts  3.68 us
    ppermute x1, starting transfers between devices, per_device(): before = lax.ppermute(own, 'seq', [(i, i + 1) for i in range(ways - 1)])  1.75 us
  transfers between devices with their start and end apart: 3, of which 2 were waited for; matrix products, arithmetic and copies ran while one was open for 2% of the time, Pallas kernels for 0%

profile of v1, /device:TPU:2, one launch (start us, length us, event | category | flops | bytes accessed | tf_op | source)
XLA Modules:
  0.0 75.0 jit_solution(13487859653944628339)
XLA Ops:
  0.6 1.0 %pad_maximum_fusion.kc_ref.vc_ref = bf16[128,1024]{1,0:T(8,128)(2,1)S(1)} fusion(bf16[128,512]{1,0:T(8,128)(2,1)} %bitcast.15, bf16[128,512]{1,0:T(8,128)(2,1)} %bitcast.16), kind=kLoop, calls=%fused_computation.1 | loop fusion | flops 524288 | bytes 524288 | tf_op jit(solution)/shard_map/concatenate | solution.py:157
  1.6 1.8 %collective-permute-start = (bf16[128,1024]{1,0:T(8,128)(2,1)S(1)}, bf16[128,1024]{1,0:T(8,128)(2,1)S(1)}, u32[]{:S(2)}, u32[]{:S(2)}) collective-permute-start(bf16[128,1024]{1,0:T(8,128)(2,1)S(1)} %pad_maximum_fusion.kc_ref.vc_ref), channel_id=1, source_target_pairs={{0,32},{32,64},{64,96},{96,128},{128,160},{160,192},{192,224},{224... | collective-permute-start | bytes 786440 | tf_op jit(solution)/shard_map/ppermute | solution.py:158
  3.4 0.0 copy-start.3
  3.4 1.1 %collective-permute-done.kp_ref.vp_ref = bf16[128,1024]{1,0:T(8,128)(2,1)S(1)} collective-permute-done((bf16[128,1024]{1,0:T(8,128)(2,1)S(1)}, bf16[128,1024]{1,0:T(8,128)(2,1)S(1)}, u32[]{:S(2)}, u32[]{:S(2)}) %collective-permute-start) | collective-permute-done | bytes 262176 | tf_op jit(solution)/shard_map/ppermute | solution.py:158
  4.5 0.0 copy-done.3
  4.5 0.0 copy-start
  4.5 1.2 %copy-done = bf16[1,128,4096]{2,1,0:T(8,128)(2,1)S(1)} copy-done((bf16[1,128,4096]{2,1,0:T(8,128)(2,1)S(1)}, bf16[1,128,4096]{2,1,0:T(8,128)(2,1)}, u32[]{:S(2)}) %copy-start) | copy-done | bytes 1048600
  5.7 0.0 copy-start.1
  5.7 1.2 %copy-done.1 = bf16[1,128,4096]{2,1,0:T(8,128)(2,1)S(1)} copy-done((bf16[1,128,4096]{2,1,0:T(8,128)(2,1)S(1)}, bf16[1,128,4096]{2,1,0:T(8,128)(2,1)}, u32[]{:S(2)}) %copy-start.1) | copy-done | bytes 1048600
  7.0 0.0 copy-start.2
  7.0 1.2 %copy-done.2 = bf16[1,128,4096]{2,1,0:T(8,128)(2,1)S(1)} copy-done((bf16[1,128,4096]{2,1,0:T(8,128)(2,1)S(1)}, bf16[1,128,4096]{2,1,0:T(8,128)(2,1)}, u32[]{:S(2)}) %copy-start.2) | copy-done | bytes 1048600
  8.2 9.7 %shard_map.93 = (bf16[128,4096]{1,0:T(8,128)(2,1)}, f32[2,128,512]{2,1,0:T(8,128)S(1)}, f32[2,128,512]{2,1,0:T(8,128)S(1)}, f32[40,128]{1,0:T(8,128)S(1)}) custom-call(s32[1]{0:T(128)} %bitcast.me_ref, s32[16,128]{1,0:T(8,128)S(1)} %bitcast.13, bf16[128,4096]{1,0:T(8,128)(2,1)S(1)} %bitcast.10, bf16[128,4096]{1,0:T(8,128)(2,1)S(1)} %bitcast.11, ...), custom_call_target="tpu_custom_call" | custom-call | flops 1342177280 | bytes 5242880 | tf_op jit(solution)/shard_map/pallas_call | solution.py:92
  17.9 1.3 %collective-permute-start.1 = (f32[2,128,512]{2,1,0:T(8,128)S(1)}, f32[2,128,512]{2,1,0:T(8,128)S(1)}, u32[]{:S(2)}, u32[]{:S(2)}) collective-permute-start(f32[2,128,512]{2,1,0:T(8,128)S(1)} %get-tuple-element.10), channel_id=1, source_target_pairs={{32,0},{64,32},{96,64},{128,96},{160,128},{192,160},{224,192},{256... | collective-permute-start | bytes 1572872 | tf_op jit(solution)/shard_map/ppermute | solution.py:163
  19.2 6.1 %all-gather = f32[80,128]{1,0:T(8,128)S(1)} all-gather(f32[40,128]{1,0:T(8,128)S(1)} %get-tuple-element.11), channel_id=2, replica_groups={{0,32},{64,96},{128,160},{192,224},{256,288},{320,352},{384,416},{448,4..., dimensions={0}, use_global_device_ids=true | all-gather | bytes 61440 | tf_op jit(solution)/shard_map/all_gather | solution.py:139
  25.3 19.7 %all_to_all.15 = f32[8,40,128]{2,1,0:T(8,128)S(1)} all-to-all(f32[8,40,128]{2,1,0:T(8,128)S(1)} %broadcast_in_dim.9), channel_id=1, replica_groups={{0,64,128,192,256,320,384,448},{32,96,160,224,288,352,416,480},{1,65,12..., dimensions={0} | all-to-all | bytes 327680 | tf_op jit(solution)/shard_map/all_to_all | solution.py:142
  45.0 8.9 %all_to_all.16 = f32[4,40,128]{2,1,0:T(8,128)S(1)} all-to-all(f32[4,40,128]{2,1,0:T(8,128)S(1)} %broadcast_in_dim.10), channel_id=1, replica_groups={{0,1,2,3},{4,5,6,7},{8,9,10,11},{12,13,14,15},{16,17,18,19},{20,21,22,2..., dimensions={0} | all-to-all | bytes 163840 | tf_op jit(solution)/shard_map/all_to_all | solution.py:142
  53.9 0.7 broadcast_in_dim.11
  54.6 10.3 %all-to-all-start.2 = ((f32[8,40,128]{2,1,0:T(8,128)}), f32[8,40,128]{2,1,0:T(8,128)S(1)}, u32[]{:S(2)}, u32[]{:S(2)}) async-start(f32[8,40,128]{2,1,0:T(8,128)} %broadcast_in_dim.11), calls=%async_computation.2 | async-start | bytes 327680 | tf_op jit(solution)/shard_map/all_to_all | solution.py:142
  64.9 0.0 collective-permute-done.1
  64.9 0.1 add_convert_fusion
  65.0 0.7 fusion
  65.7 8.6 %all-to-all-done.2 = f32[8,40,128]{2,1,0:T(8,128)S(1)} async-done(((f32[8,40,128]{2,1,0:T(8,128)}), f32[8,40,128]{2,1,0:T(8,128)S(1)}, u32[]{:S(2)}, u32[]{:S(2)}) %all-to-all-start.2) | async-done | bytes 163872 | tf_op jit(solution)/shard_map/all_to_all | solution.py:142
  74.3 0.6 reduce_sum.39
  (5 shorter events, 0.1 us)
Async XLA Ops:
  1.6 2.9 %collective-permute-start = (bf16[128,1024]{1,0:T(8,128)(2,1)S(1)}, bf16[128,1024]{1,0:T(8,128)(2,1)S(1)}, u32[]{:S(2)}, u32[]{:S(2)}) collective-permute-start(bf16[128,1024]{1,0:T(8,128)(2,1)S(1)} %pad_maximum_fusion.kc_ref.vc_ref), channel_id=1, source_target_pairs={{0,32},{32,64},{64,96},{96,128},{128,160},{160,192},{192,224},{224... | collective-permute-start | bytes 786440 | tf_op jit(solution)/shard_map/ppermute | solution.py:158
  3.4 1.1 %copy-start.3 = (s32[1,2048]{1,0:T(1,128)S(1)}, s32[1,2048]{1,0:T(1,128)}, u32[]{:S(2)}) copy-start(s32[1,2048]{1,0:T(1,128)} %param.11) | copy-start | bytes 24580
  4.5 1.2 %copy-start = (bf16[1,128,4096]{2,1,0:T(8,128)(2,1)S(1)}, bf16[1,128,4096]{2,1,0:T(8,128)(2,1)}, u32[]{:S(2)}) copy-start(bf16[1,128,4096]{2,1,0:T(8,128)(2,1)} %param.6) | copy-start | bytes 3145732
  5.7 1.2 %copy-start.1 = (bf16[1,128,4096]{2,1,0:T(8,128)(2,1)S(1)}, bf16[1,128,4096]{2,1,0:T(8,128)(2,1)}, u32[]{:S(2)}) copy-start(bf16[1,128,4096]{2,1,0:T(8,128)(2,1)} %param.9) | copy-start | bytes 3145732
  7.0 1.2 %copy-start.2 = (bf16[1,128,4096]{2,1,0:T(8,128)(2,1)S(1)}, bf16[1,128,4096]{2,1,0:T(8,128)(2,1)}, u32[]{:S(2)}) copy-start(bf16[1,128,4096]{2,1,0:T(8,128)(2,1)} %param.10) | copy-start | bytes 3145732
  17.9 47.0 %collective-permute-start.1 = (f32[2,128,512]{2,1,0:T(8,128)S(1)}, f32[2,128,512]{2,1,0:T(8,128)S(1)}, u32[]{:S(2)}, u32[]{:S(2)}) collective-permute-start(f32[2,128,512]{2,1,0:T(8,128)S(1)} %get-tuple-element.10), channel_id=1, source_target_pairs={{32,0},{64,32},{96,64},{128,96},{160,128},{192,160},{224,192},{256... | collective-permute-start | bytes 1572872 | tf_op jit(solution)/shard_map/ppermute | solution.py:163
  54.6 19.7 %all-to-all-start.2 = ((f32[8,40,128]{2,1,0:T(8,128)}), f32[8,40,128]{2,1,0:T(8,128)S(1)}, u32[]{:S(2)}, u32[]{:S(2)}) async-start(f32[8,40,128]{2,1,0:T(8,128)} %broadcast_in_dim.11), calls=%async_computation.2 | async-start | bytes 327680 | tf_op jit(solution)/shard_map/all_to_all | solution.py:142

commit v2 on v1

v2 whole, which is shorter than its diff:
```python
import math

import jax
import jax.numpy as jnp
from jax import lax
from jax.experimental import pallas as pl
from jax.experimental.pallas import tpu as pltpu
from jax.sharding import PartitionSpec as P

HD = 128
ROWS = 128
GROUP = 8
NEG = -1e30
SCALE = 1.0 / math.sqrt(HD)
SCALE2 = SCALE * math.log2(math.e)
NT = (((1,), (1,)), ((), ()))
NN = (((1,), (0,)), ((), ()))


def dot(a, b, dims=NN):
    return lax.dot_general(a, b, dims, preferred_element_type=jnp.float32)


def column(row):
    key = lax.broadcasted_iota(jnp.int32, (ROWS, ROWS), 0)
    at = lax.broadcasted_iota(jnp.int32, (ROWS, ROWS), 1)
    return jnp.sum(jnp.where(key == at, jnp.broadcast_to(row, (ROWS, ROWS)), 0), axis=1, keepdims=True)


def heads(width=HD):
    return [slice(h * width, (h + 1) * width) for h in range(GROUP)]


def own_kernel(
    me_ref, seg_ref, q_ref, o_ref, do_ref, k_ref, v_ref,
    power_ref, slope_ref, qs_ref, dos_ref, ks_ref, stat_ref, before_mask_ref, mask_ref,
):
    group = pl.program_id(0)

    @pl.when(group == 0)
    def _():
        me = me_ref[0]
        seg = seg_ref[pl.ds(me, 1), :]
        seg_before = seg_ref[pl.ds(jnp.maximum(me - 1, 0), 1), :]
        key = lax.broadcasted_iota(jnp.int32, (ROWS, ROWS), 0)
        row = lax.broadcasted_iota(jnp.int32, (ROWS, ROWS), 1)
        mask_ref[...] = jnp.where((column(seg) == seg) & (key <= row), 0.0, NEG)
        before_mask_ref[...] = jnp.where((column(seg_before) == seg) & (me > 0), 0.0, NEG)

    mask = mask_ref[...]
    q_all = jnp.concatenate([q_ref[:, at] for at in heads()], axis=0)
    do_all = jnp.concatenate([do_ref[:, at] for at in heads()], axis=0)
    qs_ref[group] = q_all
    dos_ref[group] = do_all
    ks_ref[group] = k_ref[...]
    scores_all = dot(k_ref[...], q_all, NT)
    grads_all = dot(v_ref[...], do_all, NT)
    for at in heads():
        products = do_ref[:, at].astype(jnp.float32) * o_ref[:, at].astype(jnp.float32)
        delta = jnp.sum(products.T, axis=0, keepdims=True)
        scores = scores_all[:, at] * SCALE2 + mask
        peak = jnp.max(scores, axis=0, keepdims=True)
        powers = jnp.exp2(scores - peak)
        power_ref[group, :, at] = powers
        slope_ref[group, :, at] = powers * (grads_all[:, at] - delta)
        stat_ref[group, 0:1, at] = peak
        stat_ref[group, 1:2, at] = jnp.sum(powers, axis=0, keepdims=True)
        stat_ref[group, 2:3, at] = delta


def whole_kernel(
    power_ref, slope_ref, qs_ref, dos_ref, ks_ref, stat_ref, mask_ref, k_before_ref, v_before_ref,
    dq_ref, kept_ref, back_ref, sums_ref,
    w_ref, ds_ref, dq_buf, sems,
):
    shared = power_ref.shape[0]
    mask = mask_ref[...]
    copies = []
    for group in range(shared):
        k_at = slice(group * HD, (group + 1) * HD)
        k_before = k_before_ref[:, k_at]
        v_before = v_before_ref[:, k_at]
        keys_t = jnp.concatenate([k_before, ks_ref[group]], axis=0).T
        q_all = qs_ref[group]
        do_all = dos_ref[group]
        scores_all = dot(k_before, q_all, NT)
        grads_all = dot(v_before, do_all, NT)
        for at in heads():
            peak_own = stat_ref[group, 0:1, at]
            scores = scores_all[:, at] * SCALE2 + mask
            peak = jnp.maximum(jnp.max(scores, axis=0, keepdims=True), peak_own)
            powers = jnp.exp2(scores - peak)
            fade = jnp.exp2(peak_own - peak)
            total = jnp.sum(powers, axis=0, keepdims=True) + stat_ref[group, 1:2, at] * fade
            share = 1.0 / total
            weights = powers * share
            share_own = fade * share
            w_ref[group, 0:ROWS, at] = weights.astype(jnp.bfloat16)
            w_ref[group, ROWS:, at] = (power_ref[group, :, at] * share_own).astype(jnp.bfloat16)
            ds_ref[group, 0:ROWS, at] = (weights * (grads_all[:, at] - stat_ref[group, 2:3, at])).astype(jnp.bfloat16)
            ds_ref[group, ROWS:, at] = (slope_ref[group, :, at] * share_own).astype(jnp.bfloat16)
        dq_t = (dot(keys_t, ds_ref[group]) * SCALE).astype(jnp.bfloat16)
        for head, at in enumerate(heads()):
            dq = dq_t[:, at].T
            dq_buf[group, :, at] = dq
            row = group * GROUP + head
            sums_ref[row : row + 1, :] = jnp.sum(dq.astype(jnp.float32), axis=0, keepdims=True)
        copies.append(
            pltpu.make_async_copy(
                dq_buf.at[group], dq_ref.at[:, pl.ds(group * GROUP * HD, GROUP * HD)], sems.at[group]
            )
        )
        copies[-1].start()
        key_part = dot(ds_ref[group], q_all) * SCALE
        value_part = dot(w_ref[group], do_all)
        back_ref[0, :, k_at] = key_part[:ROWS]
        back_ref[1, :, k_at] = value_part[:ROWS]
        kept_ref[0, :, k_at] = key_part[ROWS:]
        kept_ref[1, :, k_at] = value_part[ROWS:]
        base = shared * GROUP + group
        sums_ref[base : base + 1, :] = jnp.sum(key_part, axis=0, keepdims=True)
        sums_ref[base + shared : base + shared + 1, :] = jnp.sum(value_part, axis=0, keepdims=True)
    for copy in copies:
        copy.wait()


VMEM = pl.BlockSpec(memory_space=pltpu.VMEM)
SMEM = pl.BlockSpec(memory_space=pltpu.SMEM)


def own_part(me, segments, queries, forward_out, out_grad, keys, values):
    shared = keys.shape[1] // HD
    wide = pl.BlockSpec((ROWS, GROUP * HD), lambda g: (0, g))
    narrow = pl.BlockSpec((ROWS, HD), lambda g: (0, g))
    hbm = [pltpu.with_memory_space_constraint(x, pltpu.HBM) for x in (queries, forward_out, out_grad, keys, values)]
    terms = (shared, ROWS, GROUP * ROWS)
    stacked = (shared, GROUP * ROWS, HD)
    return pl.pallas_call(
        own_kernel,
        grid=(shared,),
        in_specs=[SMEM, pl.BlockSpec(segments.shape, lambda g: (0, 0)), wide, wide, wide, narrow, narrow],
        out_specs=[VMEM] * 7,
        out_shape=[
            pltpu.VMEM(terms, jnp.float32),
            pltpu.VMEM(terms, jnp.float32),
            pltpu.VMEM(stacked, jnp.bfloat16),
            pltpu.VMEM(stacked, jnp.bfloat16),
            pltpu.VMEM((shared, ROWS, HD), jnp.bfloat16),
            pltpu.VMEM((shared, 8, GROUP * ROWS), jnp.float32),
            pltpu.VMEM((ROWS, ROWS), jnp.float32),
        ],
        scratch_shapes=[pltpu.VMEM((ROWS, ROWS), jnp.float32)],
        compiler_params=pltpu.CompilerParams(vmem_limit_bytes=24 * 1024 * 1024),
        cost_estimate=pl.CostEstimate(
            flops=4 * 2 * ROWS * ROWS * HD * shared * GROUP,
            bytes_accessed=4 * 1024 * 1024,
            transcendentals=ROWS * ROWS * shared * GROUP,
        ),
    )(me, pltpu.with_memory_space_constraint(segments, pltpu.HBM), *hbm)


def whole_part(terms, keys_before, values_before):
    shared = keys_before.shape[1] // HD
    sum_rows = shared * GROUP + 2 * shared
    pinned = [pltpu.with_memory_space_constraint(x, pltpu.VMEM) for x in (*terms, keys_before, values_before)]
    return pl.pallas_call(
        whole_kernel,
        in_specs=[VMEM] * 9,
        out_specs=[pl.BlockSpec(memory_space=pltpu.HBM), VMEM, VMEM, VMEM],
        out_shape=[
            jax.ShapeDtypeStruct((ROWS, shared * GROUP * HD), jnp.bfloat16),
            pltpu.VMEM((2, ROWS, shared * HD), jnp.float32),
            pltpu.VMEM((2, ROWS, shared * HD), jnp.float32),
            pltpu.VMEM((sum_rows, HD), jnp.float32),
        ],
        scratch_shapes=[
            pltpu.VMEM((shared, 2 * ROWS, GROUP * ROWS), jnp.bfloat16),
            pltpu.VMEM((shared, 2 * ROWS, GROUP * ROWS), jnp.bfloat16),
            pltpu.VMEM((shared, ROWS, GROUP * HD), jnp.bfloat16),
            pltpu.SemaphoreType.DMA((shared,)),
        ],
        compiler_params=pltpu.CompilerParams(vmem_limit_bytes=32 * 1024 * 1024),
        cost_estimate=pl.CostEstimate(
            flops=7 * 2 * ROWS * ROWS * HD * shared * GROUP,
            bytes_accessed=3 * 1024 * 1024,
            transcendentals=ROWS * ROWS * shared * GROUP,
        ),
    )(*pinned)


def group_sum(x, masks):
    span = [0]
    for m in masks:
        span = span + [a ^ m for a in span]
    groups, seen = [], set()
    for i in range(lax.axis_size("seq") * lax.axis_size("dp")):
        if i not in seen:
            groups.append(sorted(i ^ a for a in span))
            seen |= set(groups[-1])
    copies = jnp.broadcast_to(x[None], (len(span),) + x.shape)
    parts = lax.all_to_all(
        copies, ("seq", "dp"), split_axis=0, concat_axis=0, tiled=True, axis_index_groups=groups
    )
    return jnp.sum(parts, axis=0)


def bits(low, high):
    return [low << i for i in range((high // low).bit_length() - 1)]


def per_device(queries, key_vectors, value_vectors, forward_out, out_grad, segment_number):
    ways = lax.axis_size("seq")
    me = lax.axis_index("seq").astype(jnp.int32).reshape(1)
    onward = [(i, i + 1) for i in range(ways - 1)]
    keys_before = lax.ppermute(key_vectors[0], "seq", onward)
    values_before = lax.ppermute(value_vectors[0], "seq", onward)
    segments = segment_number.reshape(ways, ROWS)
    terms = own_part(
        me, segments, queries[0], forward_out[0], out_grad[0], key_vectors[0], value_vectors[0]
    )
    query_grad, kept, back, sums = whole_part(terms, keys_before, values_before)
    low = back.astype(jnp.bfloat16)
    returned = lax.ppermute(low, "seq", [(i + 1, i) for i in range(ways - 1)])
    places = lax.axis_size("dp")
    sums = group_sum(sums, bits(2 * places, ways * places))
    both = (kept + returned.astype(jnp.float32)).astype(jnp.bfloat16)
    sums = group_sum(sums, [places] + bits(1, 4))
    sums = group_sum(sums, bits(4, places))
    return (query_grad[None], both[0][None], both[1][None], sums.reshape(-1))


def solution(mesh):
    rows = P("dp", "seq", None)
    return jax.shard_map(
        per_device,
        mesh=mesh,
        in_specs=(rows, rows, rows, rows, rows, P("dp", None)),
        out_specs=(rows, rows, rows, P()),
        check_vma=False,
    )
```

time: 75.4 us -> 63.3 us (0.84)
  blocking collectives: 34.7 us -> 9.43 us
  starting transfers between devices: 13.3 us -> 24.6 us
  waiting for transfers between devices: 9.72 us -> 17.4 us
  local copies, waits for them, and re-layouts: 5.08 us -> 2.06 us
  Pallas kernels: 9.69 us -> 7.91 us
  other arithmetic: 1.73 us -> 0.75 us
    all_to_all x2 -> x1, blocking collectives: 28.6 us -> 9.43 us  [group_sum(): lax.all_to_all(copies, ('seq', 'dp'), split_axis=0, concat_axis=0, tiled=...]
    all_to_all x1 -> x2, waiting for transfers between devices: 8.61 us -> 17.3 us  [group_sum(): lax.all_to_all(copies, ('seq', 'dp'), split_axis=0, concat_axis=0, tiled=...]
    all_to_all x1 -> x2, starting transfers between devices: 10.3 us -> 17.8 us  [group_sum(): lax.all_to_all(copies, ('seq', 'dp'), split_axis=0, concat_axis=0, tiled=...]
    all_gather x1 -> x0, blocking collectives: 6.13 us -> none  [group_sum(): parts = lax.all_gather(x, axis, axis_index_groups=groups)]
    ppermute x2 -> x3, starting transfers between devices: 3.03 us -> 6.8 us  [the longest x1 3.76 us: per_device(): values_before = lax.ppermute(value_vectors[0], 'seq', onward)]
    unnamed x8 -> x0, local copies, waits for them, and re-layouts: 3.68 us -> none
    pallas_call x1 -> x2, Pallas kernels: 9.69 us -> 7.91 us  [the longest x1 4.21 us: whole_part(): pl.pallas_call(whole_kernel, in_specs=[VMEM] * 9, out_specs=[pl.BlockSpec...]
    ppermute x2 -> x3, waiting for transfers between devices: 1.12 us -> 0.01 us  [the longest x1 0.01 us: per_device(): returned = lax.ppermute(low, 'seq', [(i + 1, i) for i in range(ways - 1)])]
  transfers between devices with their start and end apart: 3 -> 5, of which waited for: 2 -> 2; matrix products, arithmetic and copies ran while one was open for 2% -> 2% of each run, Pallas kernels for 0% -> 6%
where the time goes in v2:
time: 63.3 us; the launch traced here: 62.8 us
  starting transfers between devices  24.6 us (39%)
  waiting for transfers between devices  17.4 us (27%)
  blocking collectives  9.43 us (15%)
  Pallas kernels  7.91 us (12%)
  local copies, waits for them, and re-layouts  2.06 us (3%)
  other arithmetic  0.75 us (1%)
  between operations  0.73 us (1%)
    all_to_all x2, starting transfers between devices, group_sum(): lax.all_to_all(copies, ('seq', 'dp'), split_axis=0, concat_axis=0, tiled=...  17.8 us
    all_to_all x2, waiting for transfers between devices, group_sum(): lax.all_to_all(copies, ('seq', 'dp'), split_axis=0, concat_axis=0, tiled=...  17.3 us
    all_to_all x1, blocking collectives, group_sum(): lax.all_to_all(copies, ('seq', 'dp'), split_axis=0, concat_axis=0, tiled=...  9.43 us
    pallas_call x1, Pallas kernels, whole_part(): pl.pallas_call(whole_kernel, in_specs=[VMEM] * 9, out_specs=[pl.BlockSpec...  4.21 us
    ppermute x1, starting transfers between devices, per_device(): values_before = lax.ppermute(value_vectors[0], 'seq', onward)  3.76 us
    pallas_call x1, Pallas kernels, own_part(): pl.pallas_call(own_kernel, grid=(shared,), in_specs=[SMEM, pl.BlockSpec(s...  3.7 us
    ppermute x1, starting transfers between devices, per_device(): keys_before = lax.ppermute(key_vectors[0], 'seq', onward)  1.75 us
    broadcast_in_dim x3, local copies, waits for them, and re-layouts, group_sum(): copies = jnp.broadcast_to(x[None], (len(span),) + x.shape)  1.34 us
  transfers between devices with their start and end apart: 5, of which 2 were waited for; matrix products, arithmetic and copies ran while one was open for 2% of the time, Pallas kernels for 6%

profile of v2, /device:TPU:2, one launch (start us, length us, event | category | flops | bytes accessed | tf_op | source)
XLA Modules:
  0.0 62.8 jit_solution(14480519181701754017)
XLA Ops:
  0.6 1.7 %collective-permute-start = (bf16[128,512]{1,0:T(8,128)(2,1)}, bf16[128,512]{1,0:T(8,128)(2,1)S(1)}, u32[]{:S(2)}, u32[]{:S(2)}) collective-permute-start(bf16[128,512]{1,0:T(8,128)(2,1)} %bitcast.12), channel_id=1, source_target_pairs={{0,32},{32,64},{64,96},{96,128},{128,160},{160,192},{192,224},{224... | collective-permute-start | bytes 393224 | tf_op jit(solution)/shard_map/ppermute | solution.py:215
  2.4 3.8 %collective-permute-start.1 = (bf16[128,512]{1,0:T(8,128)(2,1)}, bf16[128,512]{1,0:T(8,128)(2,1)S(1)}, u32[]{:S(2)}, u32[]{:S(2)}) collective-permute-start(bf16[128,512]{1,0:T(8,128)(2,1)} %bitcast.14), channel_id=1, source_target_pairs={{0,32},{32,64},{64,96},{96,128},{128,160},{160,192},{192,224},{224... | collective-permute-start | bytes 393224 | tf_op jit(solution)/shard_map/ppermute | solution.py:216
  6.2 3.7 %shard_map.93 = (f32[4,128,1024]{2,1,0:T(8,128)S(1)}, f32[4,128,1024]{2,1,0:T(8,128)S(1)}, bf16[4,1024,128]{2,1,0:T(8,128)(2,1)S(1)}, bf16[4,1024,128]{2,1,0:T(8...) custom-call(s32[1]{0:T(128)} %bitcast.me_ref, ...), custom_call_target="tpu_custom_call" | custom-call | flops 536870912 | bytes 4194304 | tf_op jit(solution)/shard_map/pallas_call | solution.py:138
  9.9 0.0 collective-permute-done.k_before_ref
  9.9 0.0 collective-permute-done.1.v_before_ref
  9.9 4.2 %shard_map.94 = (bf16[128,4096]{1,0:T(8,128)(2,1)}, f32[2,128,512]{2,1,0:T(8,128)S(1)}, f32[2,128,512]{2,1,0:T(8,128)S(1)}, f32[40,128]{1,0:T(8,128)S(1)}) custom-call(f32[4,128,1024]{2,1,0:T(8,128)S(1)} %get-tuple-element.15.power_ref, f32[4,128,1024]{2,1,0:T(8,128)S(1)} %get-tuple-element.16.slope_ref, bf16[4,1024,128]{2,1,0:T(8,128)(2,1)S(1)} %get-tuple-element.17.qs_ref, ...), custom_call_target="tpu_custom_call" | custom-call | flops 939524096 | bytes 3145728 | tf_op jit(solution)/shard_map/pallas_call | solution.py:166
  14.1 0.7 %broadcast_in_dim.9 = f32[8,40,128]{2,1,0:T(8,128)} broadcast(f32[40,128]{1,0:T(8,128)S(1)} %get-tuple-element.25), dimensions={1,2} | broadcast | bytes 184320 | tf_op jit(solution)/shard_map/broadcast_in_dim | solution.py:200
  14.8 7.5 %all-to-all-start = ((f32[8,40,128]{2,1,0:T(8,128)}), f32[8,40,128]{2,1,0:T(8,128)S(1)}, u32[]{:S(2)}, u32[]{:S(2)}) async-start(f32[8,40,128]{2,1,0:T(8,128)} %broadcast_in_dim.9), calls=%async_computation | async-start | bytes 327680 | tf_op jit(solution)/shard_map/all_to_all | solution.py:201
  22.3 1.3 %collective-permute-start.2 = (bf16[2,128,512]{2,1,0:T(8,128)(2,1)S(1)}, bf16[2,128,512]{2,1,0:T(8,128)(2,1)S(1)}, u32[]{:S(2)}, u32[]{:S(2)}) collective-permute-start(bf16[2,128,512]{2,1,0:T(8,128)(2,1)S(1)} %convert_element_type.9), channel_id=1, source_target_pairs={{32,0},{64,32},{96,64},{128,96},{160,128},{192,160},{224,192},{256... | collective-permute-start | bytes 786440 | tf_op jit(solution)/shard_map/ppermute | solution.py:223
  23.6 8.1 %all-to-all-done = f32[8,40,128]{2,1,0:T(8,128)S(1)} async-done(((f32[8,40,128]{2,1,0:T(8,128)}), f32[8,40,128]{2,1,0:T(8,128)S(1)}, u32[]{:S(2)}, u32[]{:S(2)}) %all-to-all-start) | async-done | bytes 163872 | tf_op jit(solution)/shard_map/all_to_all | solution.py:201
  31.7 9.4 %all_to_all.15 = f32[8,40,128]{2,1,0:T(8,128)S(1)} all-to-all(f32[8,40,128]{2,1,0:T(8,128)S(1)} %broadcast_in_dim.10), channel_id=1, replica_groups={{0,1,2,3,32,33,34,35},{4,5,6,7,36,37,38,39},{8,9,10,11,40,41,42,43},{12..., dimensions={0} | all-to-all | bytes 327680 | tf_op jit(solution)/shard_map/all_to_all | solution.py:201
  41.2 0.7 %broadcast_in_dim.11 = f32[8,40,128]{2,1,0:T(8,128)} broadcast(f32[40,128]{1,0:T(8,128)S(1)} %reduce_sum.28), dimensions={1,2} | broadcast | bytes 184320 | tf_op jit(solution)/shard_map/broadcast_in_dim | solution.py:200
  41.8 10.3 %all-to-all-start.2 = ((f32[8,40,128]{2,1,0:T(8,128)}), f32[8,40,128]{2,1,0:T(8,128)S(1)}, u32[]{:S(2)}, u32[]{:S(2)}) async-start(f32[8,40,128]{2,1,0:T(8,128)} %broadcast_in_dim.11), calls=%async_computation.2 | async-start | bytes 327680 | tf_op jit(solution)/shard_map/all_to_all | solution.py:201
  52.2 0.0 collective-permute-done.2
  52.2 0.1 add_convert_fusion
  52.2 0.7 %fusion = (bf16[1,128,512]{2,1,0:T(8,128)(2,1)}, bf16[1,128,512]{2,1,0:T(8,128)(2,1)}) fusion(bf16[2,128,512]{2,1,0:T(8,128)(2,1)S(1)} %add_convert_fusion), kind=kLoop, calls=%fused_computation.1 | loop fusion | bytes 524288 | tf_op jit(solution)/shard_map/slice | solution.py:229
  53.0 9.2 %all-to-all-done.2 = f32[8,40,128]{2,1,0:T(8,128)S(1)} async-done(((f32[8,40,128]{2,1,0:T(8,128)}), f32[8,40,128]{2,1,0:T(8,128)S(1)}, u32[]{:S(2)}, u32[]{:S(2)}) %all-to-all-start.2) | async-done | bytes 163872 | tf_op jit(solution)/shard_map/all_to_all | solution.py:201
  62.2 0.6 reduce_sum.29
  (4 shorter events, 0.1 us)
Async XLA Ops:
  0.6 9.2 %collective-permute-start = (bf16[128,512]{1,0:T(8,128)(2,1)}, bf16[128,512]{1,0:T(8,128)(2,1)S(1)}, u32[]{:S(2)}, u32[]{:S(2)}) collective-permute-start(bf16[128,512]{1,0:T(8,128)(2,1)} %bitcast.12), channel_id=1, source_target_pairs={{0,32},{32,64},{64,96},{96,128},{128,160},{160,192},{192,224},{224... | collective-permute-start | bytes 393224 | tf_op jit(solution)/shard_map/ppermute | solution.py:215
  2.4 7.5 %collective-permute-start.1 = (bf16[128,512]{1,0:T(8,128)(2,1)}, bf16[128,512]{1,0:T(8,128)(2,1)S(1)}, u32[]{:S(2)}, u32[]{:S(2)}) collective-permute-start(bf16[128,512]{1,0:T(8,128)(2,1)} %bitcast.14), channel_id=1, source_target_pairs={{0,32},{32,64},{64,96},{96,128},{128,160},{160,192},{192,224},{224... | collective-permute-start | bytes 393224 | tf_op jit(solution)/shard_map/ppermute | solution.py:216
  14.8 16.9 %all-to-all-start = ((f32[8,40,128]{2,1,0:T(8,128)}), f32[8,40,128]{2,1,0:T(8,128)S(1)}, u32[]{:S(2)}, u32[]{:S(2)}) async-start(f32[8,40,128]{2,1,0:T(8,128)} %broadcast_in_dim.9), calls=%async_computation | async-start | bytes 327680 | tf_op jit(solution)/shard_map/all_to_all | solution.py:201
  22.3 29.9 %collective-permute-start.2 = (bf16[2,128,512]{2,1,0:T(8,128)(2,1)S(1)}, bf16[2,128,512]{2,1,0:T(8,128)(2,1)S(1)}, u32[]{:S(2)}, u32[]{:S(2)}) collective-permute-start(bf16[2,128,512]{2,1,0:T(8,128)(2,1)S(1)} %convert_element_type.9), channel_id=1, source_target_pairs={{32,0},{64,32},{96,64},{128,96},{160,128},{192,160},{224,192},{256... | collective-permute-start | bytes 786440 | tf_op jit(solution)/shard_map/ppermute | solution.py:223
  41.8 20.4 %all-to-all-start.2 = ((f32[8,40,128]{2,1,0:T(8,128)}), f32[8,40,128]{2,1,0:T(8,128)S(1)}, u32[]{:S(2)}, u32[]{:S(2)}) async-start(f32[8,40,128]{2,1,0:T(8,128)} %broadcast_in_dim.11), calls=%async_computation.2 | async-start | bytes 327680 | tf_op jit(solution)/shard_map/all_to_all | solution.py:201

commit v3 on v2

v3 whole, which is shorter than its diff:
```python
import math

import jax
import jax.numpy as jnp
from jax import lax
from jax.experimental import pallas as pl
from jax.experimental.pallas import tpu as pltpu
from jax.sharding import PartitionSpec as P

HD = 128
ROWS = 128
GROUP = 8
NEG = -1e30
SCALE = 1.0 / math.sqrt(HD)
SCALE2 = SCALE * math.log2(math.e)
NT = (((1,), (1,)), ((), ()))
NN = (((1,), (0,)), ((), ()))
TN = (((0,), (0,)), ((), ()))


VMEM = pl.BlockSpec(memory_space=pltpu.VMEM)
SMEM = pl.BlockSpec(memory_space=pltpu.SMEM)
HBM = pl.BlockSpec(memory_space=pltpu.HBM)


def dot(a, b, dims=NN):
    return lax.dot_general(a, b, dims, preferred_element_type=jnp.float32)


def column(row):
    key = lax.broadcasted_iota(jnp.int32, (ROWS, ROWS), 0)
    at = lax.broadcasted_iota(jnp.int32, (ROWS, ROWS), 1)
    return jnp.sum(jnp.where(key == at, jnp.broadcast_to(row, (ROWS, ROWS)), 0), axis=1, keepdims=True)


def heads(width=HD):
    return [slice(h * width, (h + 1) * width) for h in range(GROUP)]


def own_kernel(
    me_ref, seg_hbm, q_hbm, o_hbm, do_hbm, k_hbm, v_hbm,
    power_ref, slope_ref, qs_ref, dos_ref, keys_ref, stat_ref, before_mask_ref,
    seg_ref, q_ref, o_ref, do_ref, v_ref, sems,
):
    shared = power_ref.shape[0]
    first = [
        pltpu.make_async_copy(src, dst, sems.at[3 * shared + n])
        for n, (src, dst) in enumerate(((seg_hbm, seg_ref), (k_hbm, keys_ref), (v_hbm, v_ref)))
    ]
    for copy in first:
        copy.start()
    copies = []
    for group in range(shared):
        at = pl.ds(group * GROUP * HD, GROUP * HD)
        copies.append(
            [
                pltpu.make_async_copy(src.at[:, at], dst.at[:, at], sems.at[3 * group + n])
                for n, (src, dst) in enumerate(((q_hbm, q_ref), (do_hbm, do_ref), (o_hbm, o_ref)))
            ]
        )
        for copy in copies[-1]:
            copy.start()
    for copy in first:
        copy.wait()
    me = me_ref[0]
    seg = seg_ref[pl.ds(me, 1), :]
    seg_before = seg_ref[pl.ds(jnp.maximum(me - 1, 0), 1), :]
    key = lax.broadcasted_iota(jnp.int32, (ROWS, ROWS), 0)
    row = lax.broadcasted_iota(jnp.int32, (ROWS, ROWS), 1)
    mask = jnp.where((column(seg) == seg) & (key <= row), 0.0, NEG)
    before_mask_ref[...] = jnp.where((column(seg_before) == seg) & (me > 0), 0.0, NEG)
    for group in range(shared):
        for copy in copies[group]:
            copy.wait()
        cols = [slice((group * GROUP + h) * HD, (group * GROUP + h + 1) * HD) for h in range(GROUP)]
        q_all = jnp.concatenate([q_ref[:, c] for c in cols], axis=0)
        do_all = jnp.concatenate([do_ref[:, c] for c in cols], axis=0)
        qs_ref[group] = q_all
        dos_ref[group] = do_all
        mine = slice(group * HD, (group + 1) * HD)
        scores_all = dot(keys_ref[:, mine], q_all, NT)
        grads_all = dot(v_ref[:, mine], do_all, NT)
        for c, at in zip(cols, heads()):
            products = do_ref[:, c].astype(jnp.float32) * o_ref[:, c].astype(jnp.float32)
            delta = jnp.sum(products.T, axis=0, keepdims=True)
            scores = scores_all[:, at] * SCALE2 + mask
            peak = jnp.max(scores, axis=0, keepdims=True)
            powers = jnp.exp2(scores - peak)
            power_ref[group, :, at] = powers
            slope_ref[group, :, at] = powers * (grads_all[:, at] - delta)
            stat_ref[group, 0:1, at] = peak
            stat_ref[group, 1:2, at] = jnp.sum(powers, axis=0, keepdims=True)
            stat_ref[group, 2:3, at] = delta


def weight_kernel(
    power_ref, slope_ref, qs_ref, dos_ref, stat_ref, mask_ref, k_before_ref,
    weight_ref, ds_own_ref, kept_ref, back_ref, sums_ref,
    w_ref,
):
    shared = power_ref.shape[0]
    mask = mask_ref[...]
    for group in range(shared):
        mine = slice(group * HD, (group + 1) * HD)
        scores_all = dot(k_before_ref[:, mine], qs_ref[group], NT)
        for at in heads():
            peak_own = stat_ref[group, 0:1, at]
            scores = scores_all[:, at] * SCALE2 + mask
            peak = jnp.maximum(jnp.max(scores, axis=0, keepdims=True), peak_own)
            powers = jnp.exp2(scores - peak)
            fade = jnp.exp2(peak_own - peak)
            total = jnp.sum(powers, axis=0, keepdims=True) + stat_ref[group, 1:2, at] * fade
            share = 1.0 / total
            weights = powers * share
            share_own = fade * share
            weight_ref[group, :, at] = weights
            w_ref[group, 0:ROWS, at] = weights.astype(jnp.bfloat16)
            w_ref[group, ROWS:, at] = (power_ref[group, :, at] * share_own).astype(jnp.bfloat16)
            ds_own_ref[group, :, at] = (slope_ref[group, :, at] * share_own).astype(jnp.bfloat16)
        value_part = dot(w_ref[group], dos_ref[group])
        back_ref[:, mine] = value_part[:ROWS].astype(jnp.bfloat16)
        kept_ref[:, mine] = value_part[ROWS:]
        sums_ref[group : group + 1, :] = jnp.sum(value_part, axis=0, keepdims=True)


def score_kernel(
    weight_ref, ds_own_ref, qs_ref, dos_ref, stat_ref, keys_ref, k_before_ref, v_before_ref, value_back_ref, value_sums_ref,
    dq_ref, kept_ref, back_ref, sums_ref,
    ds_ref, dq_buf, sems,
):
    shared = weight_ref.shape[0]
    base = shared * GROUP
    back_ref[1] = value_back_ref[...]
    sums_ref[base + shared : base + 2 * shared, :] = value_sums_ref[0:shared, :]
    copies = []
    for group in range(shared):
        mine = slice(group * HD, (group + 1) * HD)
        keys = jnp.concatenate([k_before_ref[:, mine], keys_ref[:, mine]], axis=0)
        grads_all = dot(v_before_ref[:, mine], dos_ref[group], NT)
        ds_ref[group, ROWS:, :] = ds_own_ref[group]
        for at in heads():
            slope = weight_ref[group, :, at] * (grads_all[:, at] - stat_ref[group, 2:3, at])
            ds_ref[group, 0:ROWS, at] = slope.astype(jnp.bfloat16)
        for head, at in enumerate(heads()):
            dq = (dot(ds_ref[group, :, at], keys, TN) * SCALE).astype(jnp.bfloat16)
            dq_buf[group, :, at] = dq
            row = group * GROUP + head
            sums_ref[row : row + 1, :] = jnp.sum(dq.astype(jnp.float32), axis=0, keepdims=True)
        copies.append(
            pltpu.make_async_copy(
                dq_buf.at[group], dq_ref.at[:, pl.ds(group * GROUP * HD, GROUP * HD)], sems.at[group]
            )
        )
        copies[-1].start()
        key_part = dot(ds_ref[group], qs_ref[group]) * SCALE
        back_ref[0, :, mine] = key_part[:ROWS].astype(jnp.bfloat16)
        kept_ref[:, mine] = key_part[ROWS:]
        sums_ref[base + group : base + group + 1, :] = jnp.sum(key_part, axis=0, keepdims=True)
    for copy in copies:
        copy.wait()


def own_part(me, segments, queries, forward_out, out_grad, keys, values):
    shared = keys.shape[1] // HD
    hbm = [pltpu.with_memory_space_constraint(x, pltpu.HBM) for x in (segments, queries, forward_out, out_grad, keys, values)]
    terms = (shared, ROWS, GROUP * ROWS)
    stacked = (shared, GROUP * ROWS, HD)
    return pl.pallas_call(
        own_kernel,
        in_specs=[SMEM] + [HBM] * 6,
        out_specs=[VMEM] * 7,
        out_shape=[
            pltpu.VMEM(terms, jnp.float32),
            pltpu.VMEM(terms, jnp.float32),
            pltpu.VMEM(stacked, jnp.bfloat16),
            pltpu.VMEM(stacked, jnp.bfloat16),
            pltpu.VMEM(keys.shape, jnp.bfloat16),
            pltpu.VMEM((shared, 8, GROUP * ROWS), jnp.float32),
            pltpu.VMEM((ROWS, ROWS), jnp.float32),
        ],
        scratch_shapes=[
            pltpu.VMEM(segments.shape, jnp.int32),
            pltpu.VMEM(queries.shape, jnp.bfloat16),
            pltpu.VMEM(queries.shape, jnp.bfloat16),
            pltpu.VMEM(queries.shape, jnp.bfloat16),
            pltpu.VMEM(values.shape, jnp.bfloat16),
            pltpu.SemaphoreType.DMA((3 * shared + 3,)),
        ],
        compiler_params=pltpu.CompilerParams(vmem_limit_bytes=32 * 1024 * 1024),
        cost_estimate=pl.CostEstimate(
            flops=4 * 2 * ROWS * ROWS * HD * shared * GROUP,
            bytes_accessed=4 * 1024 * 1024,
            transcendentals=ROWS * ROWS * shared * GROUP,
        ),
    )(me, *hbm)


def pin(*arrays):
    return [pltpu.with_memory_space_constraint(x, pltpu.VMEM) for x in arrays]


def weight_part(terms, keys_before):
    power, slope, queries, grads, _, stats, mask = terms
    shared = power.shape[0]
    return pl.pallas_call(
        weight_kernel,
        in_specs=[VMEM] * 7,
        out_specs=[VMEM] * 5,
        out_shape=[
            pltpu.VMEM(power.shape, jnp.float32),
            pltpu.VMEM(power.shape, jnp.bfloat16),
            pltpu.VMEM(keys_before.shape, jnp.float32),
            pltpu.VMEM(keys_before.shape, jnp.bfloat16),
            pltpu.VMEM((8, HD), jnp.float32),
        ],
        scratch_shapes=[pltpu.VMEM((shared, 2 * ROWS, GROUP * ROWS), jnp.bfloat16)],
        compiler_params=pltpu.CompilerParams(vmem_limit_bytes=24 * 1024 * 1024),
        cost_estimate=pl.CostEstimate(
            flops=3 * 2 * ROWS * ROWS * HD * shared * GROUP,
            bytes_accessed=1024 * 1024,
            transcendentals=ROWS * ROWS * shared * GROUP,
        ),
    )(*pin(power, slope, queries, grads, stats, mask, keys_before))


def score_part(terms, weights, ds_own, keys_before, values_before, value_back, value_sums):
    _, _, queries, grads, keys, stats, _ = terms
    shared = weights.shape[0]
    return pl.pallas_call(
        score_kernel,
        in_specs=[VMEM] * 10,
        out_specs=[HBM, VMEM, VMEM, VMEM],
        out_shape=[
            jax.ShapeDtypeStruct((ROWS, shared * GROUP * HD), jnp.bfloat16),
            pltpu.VMEM(keys.shape, jnp.float32),
            pltpu.VMEM((2,) + keys.shape, jnp.bfloat16),
            pltpu.VMEM((shared * GROUP + 2 * shared, HD), jnp.float32),
        ],
        scratch_shapes=[
            pltpu.VMEM((shared, 2 * ROWS, GROUP * ROWS), jnp.bfloat16),
            pltpu.VMEM((shared, ROWS, GROUP * HD), jnp.bfloat16),
            pltpu.SemaphoreType.DMA((shared,)),
        ],
        compiler_params=pltpu.CompilerParams(vmem_limit_bytes=24 * 1024 * 1024),
        cost_estimate=pl.CostEstimate(
            flops=5 * 2 * ROWS * ROWS * HD * shared * GROUP,
            bytes_accessed=2 * 1024 * 1024,
            transcendentals=0,
        ),
    )(*pin(weights, ds_own, queries, grads, stats, keys, keys_before, values_before, value_back, value_sums))


def group_parts(x, masks):
    span = [0]
    for m in masks:
        span = span + [a ^ m for a in span]
    groups, seen = [], set()
    for i in range(lax.axis_size("seq") * lax.axis_size("dp")):
        if i not in seen:
            groups.append(sorted(i ^ a for a in span))
            seen |= set(groups[-1])
    copies = jnp.broadcast_to(x[None], (len(span),) + x.shape)
    return lax.all_to_all(
        copies, ("seq", "dp"), split_axis=0, concat_axis=0, tiled=True, axis_index_groups=groups
    )


def bits(low, high):
    return [low << i for i in range((high // low).bit_length() - 1)]


def closing_kernel(parts_ref, key_kept_ref, value_kept_ref, returned_ref, bias_ref, key_ref, value_ref):
    bias_ref[...] = jnp.sum(parts_ref[...], axis=0)
    key_ref[...] = (key_kept_ref[...] + returned_ref[0].astype(jnp.float32)).astype(jnp.bfloat16)
    value_ref[...] = (value_kept_ref[...] + returned_ref[1].astype(jnp.float32)).astype(jnp.bfloat16)


def closing(parts, key_kept, value_kept, returned):
    grad = jax.ShapeDtypeStruct(key_kept.shape, jnp.bfloat16)
    return pl.pallas_call(
        closing_kernel,
        in_specs=[VMEM] * 4,
        out_specs=[VMEM] * 3,
        out_shape=[jax.ShapeDtypeStruct(parts.shape[1:], jnp.float32), grad, grad],
    )(*pin(parts, key_kept, value_kept, returned))


def per_device(queries, key_vectors, value_vectors, forward_out, out_grad, segment_number):
    ways = lax.axis_size("seq")
    me = lax.axis_index("seq").astype(jnp.int32).reshape(1)
    onward = [(i, i + 1) for i in range(ways - 1)]
    keys_before = lax.ppermute(key_vectors[0], "seq", onward)
    values_before = lax.ppermute(value_vectors[0], "seq", onward)
    segments = segment_number.reshape(ways, ROWS)
    terms = own_part(
        me, segments, queries[0], forward_out[0], out_grad[0], key_vectors[0], value_vectors[0]
    )
    weights, ds_own, value_kept, value_back, value_sums = weight_part(terms, keys_before)
    query_grad, key_kept, back, sums = score_part(
        terms, weights, ds_own, keys_before, values_before, value_back, value_sums
    )
    returned = lax.ppermute(back, "seq", [(i + 1, i) for i in range(ways - 1)])
    places = lax.axis_size("dp")
    sums = jnp.sum(group_parts(sums, bits(2 * places, ways * places)), axis=0)
    sums = jnp.sum(group_parts(sums, [places] + bits(1, 4)), axis=0)
    sums, returned = lax.optimization_barrier((sums, returned))
    parts = group_parts(sums, bits(4, places))
    bias_grad, key_grad, value_grad = closing(parts, key_kept, value_kept, returned)
    return (query_grad[None], key_grad[None], value_grad[None], bias_grad.reshape(-1))


def solution(mesh):
    rows = P("dp", "seq", None)
    return jax.shard_map(
        per_device,
        mesh=mesh,
        in_specs=(rows, rows, rows, rows, rows, P("dp", None)),
        out_specs=(rows, rows, rows, P()),
        check_vma=False,
    )
```

time: 63.3 us -> 61.8 us (0.976)
  blocking collectives: 9.43 us -> 29.6 us
  starting transfers between devices: 24.6 us -> 13.1 us
  waiting for transfers between devices: 17.4 us -> 8.51 us
  local copies, waits for them, and re-layouts: 2.06 us -> 0.69 us
  Pallas kernels: 7.91 us -> 8.73 us
  other arithmetic: 0.75 us -> 0.03 us
    all_to_all x1 -> x2, blocking collectives: 9.43 us -> 29.6 us  [group_parts(): lax.all_to_all(copies, ('seq', 'dp'), split_axis=0, concat_axis=0, tiled=...]
    all_to_all x2 -> x1, starting transfers between devices: 17.8 us -> 6.35 us  [group_parts(): lax.all_to_all(copies, ('seq', 'dp'), split_axis=0, concat_axis=0, tiled=...]
    all_to_all x2 -> x1, waiting for transfers between devices: 17.3 us -> 8.5 us  [group_parts(): lax.all_to_all(copies, ('seq', 'dp'), split_axis=0, concat_axis=0, tiled=...]
    pallas_call x2 -> x4, Pallas kernels: 7.91 us -> 8.73 us  [the longest x1 2.9 us: own_part(): pl.pallas_call(own_kernel, in_specs=[SMEM] + [HBM] * 6, out_specs=[VMEM]...]
    slice x1 -> x0, local copies, waits for them, and re-layouts: 0.72 us -> none  [per_device(): return (query_grad[None], both[0][None], both[1][None], sums.reshape(-1))]
    broadcast_in_dim x3, local copies, waits for them, and re-layouts: 1.34 us -> 0.69 us  [group_parts(): copies = jnp.broadcast_to(x[None], (len(span),) + x.shape)]
  transfers between devices with their start and end apart: 5 -> 4, of which waited for: 2 -> 1; matrix products, arithmetic and copies ran while one was open for 2% -> 0% of each run, Pallas kernels for 6% -> 8%
where the time goes in v3:
time: 61.8 us; the launch traced here: 61.4 us
  blocking collectives  29.6 us (48%)
  starting transfers between devices  13.1 us (21%)
  Pallas kernels  8.73 us (14%)
  waiting for transfers between devices  8.51 us (14%)
  between operations  0.73 us (1%)
  local copies, waits for them, and re-layouts  0.69 us (1%)
    all_to_all x2, blocking collectives, group_parts(): lax.all_to_all(copies, ('seq', 'dp'), split_axis=0, concat_axis=0, tiled=...  29.6 us
    all_to_all x1, waiting for transfers between devices, group_parts(): lax.all_to_all(copies, ('seq', 'dp'), split_axis=0, concat_axis=0, tiled=...  8.5 us
    all_to_all x1, starting transfers between devices, group_parts(): lax.all_to_all(copies, ('seq', 'dp'), split_axis=0, concat_axis=0, tiled=...  6.35 us
    ppermute x1, starting transfers between devices, per_device(): values_before = lax.ppermute(value_vectors[0], 'seq', onward)  3.76 us
    pallas_call x1, Pallas kernels, own_part(): pl.pallas_call(own_kernel, in_specs=[SMEM] + [HBM] * 6, out_specs=[VMEM]...  2.9 us
    pallas_call x1, Pallas kernels, score_part(): pl.pallas_call(score_kernel, in_specs=[VMEM] * 10, out_specs=[HBM, VMEM,...  2.84 us
    pallas_call x1, Pallas kernels, weight_part(): pl.pallas_call(weight_kernel, in_specs=[VMEM] * 7, out_specs=[VMEM] * 5,...  2.25 us
    ppermute x1, starting transfers between devices, per_device(): keys_before = lax.ppermute(key_vectors[0], 'seq', onward)  1.75 us
  transfers between devices with their start and end apart: 4, of which 1 were waited for; matrix products, arithmetic and copies ran while one was open for 0% of the time, Pallas kernels for 8%

profile of v3, /device:TPU:2, one launch (start us, length us, event | category | flops | bytes accessed | tf_op | source)
XLA Modules:
  0.0 61.4 jit_solution(16217565184999570341)
XLA Ops:
  0.6 1.7 %collective-permute-start = (bf16[128,512]{1,0:T(8,128)(2,1)}, bf16[128,512]{1,0:T(8,128)(2,1)S(1)}, u32[]{:S(2)}, u32[]{:S(2)}) collective-permute-start(bf16[128,512]{1,0:T(8,128)(2,1)} %bitcast.14), channel_id=1, source_target_pairs={{0,32},{32,64},{64,96},{96,128},{128,160},{160,192},{192,224},{224... | collective-permute-start | bytes 393224 | tf_op jit(solution)/shard_map/ppermute | solution.py:292
  2.4 3.8 %collective-permute-start.1 = (bf16[128,512]{1,0:T(8,128)(2,1)}, bf16[128,512]{1,0:T(8,128)(2,1)S(1)}, u32[]{:S(2)}, u32[]{:S(2)}) collective-permute-start(bf16[128,512]{1,0:T(8,128)(2,1)} %bitcast.16), channel_id=1, source_target_pairs={{0,32},{32,64},{64,96},{96,128},{128,160},{160,192},{192,224},{224... | collective-permute-start | bytes 393224 | tf_op jit(solution)/shard_map/ppermute | solution.py:293
  6.2 2.9 %shard_map.93 = (f32[4,128,1024]{2,1,0:T(8,128)S(1)}, f32[4,128,1024]{2,1,0:T(8,128)S(1)}, bf16[4,1024,128]{2,1,0:T(8,128)(2,1)S(1)}, bf16[4,1024,128]{2,1,0:T(8...) custom-call(s32[1]{0:T(128)} %bitcast.me_ref, ...), custom_call_target="tpu_custom_call" | custom-call | flops 536870912 | bytes 4194304 | tf_op jit(solution)/shard_map/pallas_call | solution.py:168
  9.1 0.0 collective-permute-done.k_before_ref
  9.1 2.2 %shard_map.94 = (f32[4,128,1024]{2,1,0:T(8,128)S(1)}, bf16[4,128,1024]{2,1,0:T(8,128)(2,1)S(1)}, f32[128,512]{1,0:T(8,128)S(1)}, bf16[128,512]{1,0:T(8,128)(2,1)S(1)}, f32[8,128]{1,0:T(8,128)S(1)}) custom-call(f32[4,128,1024]{2,1,0:T(8,128)S(1)} %get-tuple-element.25.power_ref, f32[4,128,1024]{2,1,0:T(8,128)S(1)} %get-tuple-element.26.slope_ref, ...), custom_call_target="tpu_custom_call" | custom-call | flops 402653184 | bytes 1048576 | tf_op jit(solution)/shard_map/pallas_call | solution.py:205
  11.3 0.0 collective-permute-done.1.v_before_ref
  11.3 2.8 %shard_map.95 = (bf16[128,4096]{1,0:T(8,128)(2,1)}, f32[128,512]{1,0:T(8,128)S(1)}, bf16[2,128,512]{2,1,0:T(8,128)(2,1)S(1)}, f32[40,128]{1,0:T(8,128)S(1)}) custom-call(f32[4,128,1024]{2,1,0:T(8,128)S(1)} %get-tuple-element.31.weight_ref, bf16[4,128,1024]{2,1,0:T(8,128)(2,1)S(1)} %get-tuple-element.32.ds_own_ref, ...), custom_call_target="tpu_custom_call" | custom-call | flops 671088640 | bytes 2097152 | tf_op jit(solution)/shard_map/pallas_call | solution.py:229
  14.2 0.7 %broadcast_in_dim.13 = f32[8,40,128]{2,1,0:T(8,128)} broadcast(f32[40,128]{1,0:T(8,128)S(1)} %get-tuple-element.37), dimensions={1,2} | broadcast | bytes 184320 | tf_op jit(solution)/shard_map/broadcast_in_dim | solution.py:262
  14.8 6.4 %all-to-all-start = ((f32[8,40,128]{2,1,0:T(8,128)}), f32[8,40,128]{2,1,0:T(8,128)S(1)}, u32[]{:S(2)}, u32[]{:S(2)}) async-start(f32[8,40,128]{2,1,0:T(8,128)} %broadcast_in_dim.13), calls=%async_computation | async-start | bytes 327680 | tf_op jit(solution)/shard_map/all_to_all | solution.py:263
  21.2 1.3 %collective-permute-start.2 = (bf16[2,128,512]{2,1,0:T(8,128)(2,1)S(1)}, bf16[2,128,512]{2,1,0:T(8,128)(2,1)S(1)}, u32[]{:S(2)}, u32[]{:S(2)}) collective-permute-start(bf16[2,128,512]{2,1,0:T(8,128)(2,1)S(1)} %get-tuple-element.38), channel_id=1, source_target_pairs={{32,0},{64,32},{96,64},{128,96},{160,128},{192,160},{224,192},{256... | collective-permute-start | bytes 786440 | tf_op jit(solution)/shard_map/ppermute | solution.py:302
  22.5 8.5 %all-to-all-done = f32[8,40,128]{2,1,0:T(8,128)S(1)} async-done(((f32[8,40,128]{2,1,0:T(8,128)}), f32[8,40,128]{2,1,0:T(8,128)S(1)}, u32[]{:S(2)}, u32[]{:S(2)}) %all-to-all-start) | async-done | bytes 163872 | tf_op jit(solution)/shard_map/all_to_all | solution.py:263
  31.0 9.4 %all_to_all.15 = f32[8,40,128]{2,1,0:T(8,128)S(1)} all-to-all(f32[8,40,128]{2,1,0:T(8,128)S(1)} %broadcast_in_dim.14), channel_id=1, replica_groups={{0,1,2,3,32,33,34,35},{4,5,6,7,36,37,38,39},{8,9,10,11,40,41,42,43},{12..., dimensions={0} | all-to-all | bytes 327680 | tf_op jit(solution)/shard_map/all_to_all | solution.py:263
  40.5 0.0 collective-permute-done.2.returned_ref
  40.5 20.2 %all_to_all.16.parts_ref = f32[8,40,128]{2,1,0:T(8,128)S(1)} all-to-all(f32[8,40,128]{2,1,0:T(8,128)S(1)} %broadcast_in_dim.30), channel_id=1, replica_groups={{0,4,8,12,16,20,24,28},{1,5,9,13,17,21,25,29},{2,6,10,14,18,22,26,30},{..., dimensions={0} | all-to-all | bytes 327680 | tf_op jit(solution)/shard_map/all_to_all | solution.py:263
  60.7 0.7 %shard_map.96 = (f32[40,128]{1,0:T(8,128)}, bf16[128,512]{1,0:T(8,128)(2,1)}, bf16[128,512]{1,0:T(8,128)(2,1)}) custom-call(f32[8,40,128]{2,1,0:T(8,128)S(1)} %all_to_all.16.parts_ref, f32[128,512]{1,0:T(8,128)S(1)} %get-tuple-element.40.key_kept_ref, f32[128,512]{1,0:T(8,128)S(1)} %get-tuple-element.41.value_kept_ref, ...), custom_call_target="tpu_custom_call" | custom-call | tf_op jit(solution)/shard_map/pallas_call | solution.py:280
  (4 shorter events, 0.1 us)
Async XLA Ops:
  0.6 8.4 %collective-permute-start = (bf16[128,512]{1,0:T(8,128)(2,1)}, bf16[128,512]{1,0:T(8,128)(2,1)S(1)}, u32[]{:S(2)}, u32[]{:S(2)}) collective-permute-start(bf16[128,512]{1,0:T(8,128)(2,1)} %bitcast.14), channel_id=1, source_target_pairs={{0,32},{32,64},{64,96},{96,128},{128,160},{160,192},{192,224},{224... | collective-permute-start | bytes 393224 | tf_op jit(solution)/shard_map/ppermute | solution.py:292
  2.4 8.9 %collective-permute-start.1 = (bf16[128,512]{1,0:T(8,128)(2,1)}, bf16[128,512]{1,0:T(8,128)(2,1)S(1)}, u32[]{:S(2)}, u32[]{:S(2)}) collective-permute-start(bf16[128,512]{1,0:T(8,128)(2,1)} %bitcast.16), channel_id=1, source_target_pairs={{0,32},{32,64},{64,96},{96,128},{128,160},{160,192},{192,224},{224... | collective-permute-start | bytes 393224 | tf_op jit(solution)/shard_map/ppermute | solution.py:293
  14.8 16.1 %all-to-all-start = ((f32[8,40,128]{2,1,0:T(8,128)}), f32[8,40,128]{2,1,0:T(8,128)S(1)}, u32[]{:S(2)}, u32[]{:S(2)}) async-start(f32[8,40,128]{2,1,0:T(8,128)} %broadcast_in_dim.13), calls=%async_computation | async-start | bytes 327680 | tf_op jit(solution)/shard_map/all_to_all | solution.py:263
  21.2 19.3 %collective-permute-start.2 = (bf16[2,128,512]{2,1,0:T(8,128)(2,1)S(1)}, bf16[2,128,512]{2,1,0:T(8,128)(2,1)S(1)}, u32[]{:S(2)}, u32[]{:S(2)}) collective-permute-start(bf16[2,128,512]{2,1,0:T(8,128)(2,1)S(1)} %get-tuple-element.38), channel_id=1, source_target_pairs={{32,0},{64,32},{96,64},{128,96},{160,128},{192,160},{224,192},{256... | collective-permute-start | bytes 786440 | tf_op jit(solution)/shard_map/ppermute | solution.py:302

commit v4 on v3

--- a/solution.py
+++ b/solution.py
@@ -100,9 +100,15 @@
 ):
     shared = power_ref.shape[0]
     mask = mask_ref[...]
+    def scores_of(group):
+        return dot(k_before_ref[:, group * HD : (group + 1) * HD], qs_ref[group], NT)
+
+    ahead = scores_of(0)
     for group in range(shared):
         mine = slice(group * HD, (group + 1) * HD)
-        scores_all = dot(k_before_ref[:, mine], qs_ref[group], NT)
+        scores_all = ahead
+        if group + 1 < shared:
+            ahead = scores_of(group + 1)
         for at in heads():
             peak_own = stat_ref[group, 0:1, at]
             scores = scores_all[:, at] * SCALE2 + mask
@@ -125,24 +131,32 @@
 
 def score_kernel(
     weight_ref, ds_own_ref, qs_ref, dos_ref, stat_ref, keys_ref, k_before_ref, v_before_ref, value_back_ref, value_sums_ref,
-    dq_ref, kept_ref, back_ref, sums_ref,
-    ds_ref, dq_buf, sems,
+    dq_ref, kept_ref, back_ref, copies_ref,
+    ds_ref, dq_buf, sums_ref, sems,
 ):
     shared = weight_ref.shape[0]
     base = shared * GROUP
     back_ref[1] = value_back_ref[...]
     sums_ref[base + shared : base + 2 * shared, :] = value_sums_ref[0:shared, :]
     copies = []
+
+    def grads_of(group):
+        return dot(v_before_ref[:, group * HD : (group + 1) * HD], dos_ref[group], NT)
+
+    ahead = grads_of(0)
     for group in range(shared):
         mine = slice(group * HD, (group + 1) * HD)
         keys = jnp.concatenate([k_before_ref[:, mine], keys_ref[:, mine]], axis=0)
-        grads_all = dot(v_before_ref[:, mine], dos_ref[group], NT)
+        grads_all = ahead
+        if group + 1 < shared:
+            ahead = grads_of(group + 1)
         ds_ref[group, ROWS:, :] = ds_own_ref[group]
         for at in heads():
             slope = weight_ref[group, :, at] * (grads_all[:, at] - stat_ref[group, 2:3, at])
             ds_ref[group, 0:ROWS, at] = slope.astype(jnp.bfloat16)
+        dq_t = (dot(keys.T, ds_ref[group]) * SCALE).astype(jnp.bfloat16)
         for head, at in enumerate(heads()):
-            dq = (dot(ds_ref[group, :, at], keys, TN) * SCALE).astype(jnp.bfloat16)
+            dq = dq_t[:, at].T
             dq_buf[group, :, at] = dq
             row = group * GROUP + head
             sums_ref[row : row + 1, :] = jnp.sum(dq.astype(jnp.float32), axis=0, keepdims=True)
@@ -156,6 +170,9 @@
         back_ref[0, :, mine] = key_part[:ROWS].astype(jnp.bfloat16)
         kept_ref[:, mine] = key_part[ROWS:]
         sums_ref[base + group : base + group + 1, :] = jnp.sum(key_part, axis=0, keepdims=True)
+    for n in range(copies_ref.shape[0]):
+        copies.append(pltpu.make_async_copy(sums_ref, copies_ref.at[n], sems.at[shared + n]))
+        copies[-1].start()
     for copy in copies:
         copy.wait()
 
@@ -223,23 +240,25 @@
     )(*pin(power, slope, queries, grads, stats, mask, keys_before))
 
 
-def score_part(terms, weights, ds_own, keys_before, values_before, value_back, value_sums):
+def score_part(terms, weights, ds_own, keys_before, values_before, value_back, value_sums, peers):
     _, _, queries, grads, keys, stats, _ = terms
     shared = weights.shape[0]
+    rows = shared * GROUP + 2 * shared
     return pl.pallas_call(
         score_kernel,
         in_specs=[VMEM] * 10,
-        out_specs=[HBM, VMEM, VMEM, VMEM],
+        out_specs=[HBM, VMEM, VMEM, HBM],
         out_shape=[
             jax.ShapeDtypeStruct((ROWS, shared * GROUP * HD), jnp.bfloat16),
             pltpu.VMEM(keys.shape, jnp.float32),
             pltpu.VMEM((2,) + keys.shape, jnp.bfloat16),
-            pltpu.VMEM((shared * GROUP + 2 * shared, HD), jnp.float32),
+            jax.ShapeDtypeStruct((peers, rows, HD), jnp.float32),
         ],
         scratch_shapes=[
             pltpu.VMEM((shared, 2 * ROWS, GROUP * ROWS), jnp.bfloat16),
             pltpu.VMEM((shared, ROWS, GROUP * HD), jnp.bfloat16),
-            pltpu.SemaphoreType.DMA((shared,)),
+            pltpu.VMEM((rows, HD), jnp.float32),
+            pltpu.SemaphoreType.DMA((shared + peers,)),
         ],
         compiler_params=pltpu.CompilerParams(vmem_limit_bytes=24 * 1024 * 1024),
         cost_estimate=pl.CostEstimate(
@@ -250,7 +269,7 @@
     )(*pin(weights, ds_own, queries, grads, stats, keys, keys_before, values_before, value_back, value_sums))
 
 
-def group_parts(x, masks):
+def exchange(copies, masks):
     span = [0]
     for m in masks:
         span = span + [a ^ m for a in span]
@@ -259,10 +278,13 @@
         if i not in seen:
             groups.append(sorted(i ^ a for a in span))
             seen |= set(groups[-1])
-    copies = jnp.broadcast_to(x[None], (len(span),) + x.shape)
     return lax.all_to_all(
         copies, ("seq", "dp"), split_axis=0, concat_axis=0, tiled=True, axis_index_groups=groups
     )
+
+
+def group_parts(x, masks):
+    return exchange(jnp.broadcast_to(x[None], (1 << len(masks),) + x.shape), masks)
 
 
 def bits(low, high):
@@ -296,12 +318,12 @@
         me, segments, queries[0], forward_out[0], out_grad[0], key_vectors[0], value_vectors[0]
     )
     weights, ds_own, value_kept, value_back, value_sums = weight_part(terms, keys_before)
-    query_grad, key_kept, back, sums = score_part(
-        terms, weights, ds_own, keys_before, values_before, value_back, value_sums
+    query_grad, key_kept, back, copies = score_part(
+        terms, weights, ds_own, keys_before, values_before, value_back, value_sums, ways // 2
     )
     returned = lax.ppermute(back, "seq", [(i + 1, i) for i in range(ways - 1)])
     places = lax.axis_size("dp")
-    sums = jnp.sum(group_parts(sums, bits(2 * places, ways * places)), axis=0)
+    sums = jnp.sum(exchange(copies, bits(2 * places, ways * places)), axis=0)
     sums = jnp.sum(group_parts(sums, [places] + bits(1, 4)), axis=0)
     sums, returned = lax.optimization_barrier((sums, returned))
     parts = group_parts(sums, bits(4, places))

time: 61.8 us -> 60.3 us (0.976)
  Pallas kernels: 8.73 us -> 7.95 us
  local copies, waits for them, and re-layouts: 0.69 us -> 0.03 us
    broadcast_in_dim x3 -> x2, local copies, waits for them, and re-layouts: 0.69 us -> 0.03 us  [group_parts(): jnp.broadcast_to(x[None], (1 << len(masks),) + x.shape)]
where the time goes in v4:
time: 60.3 us; the launch traced here: 60 us
  blocking collectives  29.6 us (49%)
  starting transfers between devices  13.2 us (22%)
  waiting for transfers between devices  8.5 us (14%)
  Pallas kernels  7.95 us (13%)
  between operations  0.73 us (1%)
    all_to_all x2, blocking collectives, exchange(): lax.all_to_all(copies, ('seq', 'dp'), split_axis=0, concat_axis=0, tiled=...  29.6 us
    all_to_all x1, waiting for transfers between devices, exchange(): lax.all_to_all(copies, ('seq', 'dp'), split_axis=0, concat_axis=0, tiled=...  8.49 us
    all_to_all x1, starting transfers between devices, exchange(): lax.all_to_all(copies, ('seq', 'dp'), split_axis=0, concat_axis=0, tiled=...  6.37 us
    ppermute x1, starting transfers between devices, per_device(): values_before = lax.ppermute(value_vectors[0], 'seq', onward)  3.76 us
    pallas_call x1, Pallas kernels, own_part(): pl.pallas_call(own_kernel, in_specs=[SMEM] + [HBM] * 6, out_specs=[VMEM]...  2.9 us
    pallas_call x1, Pallas kernels, score_part(): pl.pallas_call(score_kernel, in_specs=[VMEM] * 10, out_specs=[HBM, VMEM,...  2.31 us
    pallas_call x1, Pallas kernels, weight_part(): pl.pallas_call(weight_kernel, in_specs=[VMEM] * 7, out_specs=[VMEM] * 5,...  1.99 us
    ppermute x1, starting transfers between devices, per_device(): keys_before = lax.ppermute(key_vectors[0], 'seq', onward)  1.75 us
  transfers between devices with their start and end apart: 4, of which 1 were waited for; matrix products, arithmetic and copies ran while one was open for 0% of the time, Pallas kernels for 8%

profile of v4, /device:TPU:2, one launch (start us, length us, event | category | flops | bytes accessed | tf_op | source)
XLA Modules:
  0.0 60.0 jit_solution(12006299859289845028)
XLA Ops:
  0.6 1.7 %collective-permute-start = (bf16[128,512]{1,0:T(8,128)(2,1)}, bf16[128,512]{1,0:T(8,128)(2,1)S(1)}, u32[]{:S(2)}, u32[]{:S(2)}) collective-permute-start(bf16[128,512]{1,0:T(8,128)(2,1)} %bitcast.14), channel_id=1, source_target_pairs={{0,32},{32,64},{64,96},{96,128},{128,160},{160,192},{192,224},{224... | collective-permute-start | bytes 393224 | tf_op jit(solution)/shard_map/ppermute | solution.py:314
  2.4 3.8 %collective-permute-start.1 = (bf16[128,512]{1,0:T(8,128)(2,1)}, bf16[128,512]{1,0:T(8,128)(2,1)S(1)}, u32[]{:S(2)}, u32[]{:S(2)}) collective-permute-start(bf16[128,512]{1,0:T(8,128)(2,1)} %bitcast.16), channel_id=1, source_target_pairs={{0,32},{32,64},{64,96},{96,128},{128,160},{160,192},{192,224},{224... | collective-permute-start | bytes 393224 | tf_op jit(solution)/shard_map/ppermute | solution.py:315
  6.2 2.9 %shard_map.93 = (f32[4,128,1024]{2,1,0:T(8,128)S(1)}, f32[4,128,1024]{2,1,0:T(8,128)S(1)}, bf16[4,1024,128]{2,1,0:T(8,128)(2,1)S(1)}, bf16[4,1024,128]{2,1,0:T(8...) custom-call(s32[1]{0:T(128)} %bitcast.me_ref, ...), custom_call_target="tpu_custom_call" | custom-call | flops 536870912 | bytes 4194304 | tf_op jit(solution)/shard_map/pallas_call | solution.py:185
  9.1 0.0 collective-permute-done.k_before_ref
  9.1 2.0 %shard_map.94 = (f32[4,128,1024]{2,1,0:T(8,128)S(1)}, bf16[4,128,1024]{2,1,0:T(8,128)(2,1)S(1)}, f32[128,512]{1,0:T(8,128)S(1)}, bf16[128,512]{1,0:T(8,128)(2,1)S(1)}, f32[8,128]{1,0:T(8,128)S(1)}) custom-call(f32[4,128,1024]{2,1,0:T(8,128)S(1)} %get-tuple-element.25.power_ref, f32[4,128,1024]{2,1,0:T(8,128)S(1)} %get-tuple-element.26.slope_ref, ...), custom_call_target="tpu_custom_call" | custom-call | flops 402653184 | bytes 1048576 | tf_op jit(solution)/shard_map/pallas_call | solution.py:222
  11.1 0.0 collective-permute-done.1.v_before_ref
  11.1 2.3 %shard_map.95 = (bf16[128,4096]{1,0:T(8,128)(2,1)}, f32[128,512]{1,0:T(8,128)S(1)}, bf16[2,128,512]{2,1,0:T(8,128)(2,1)S(1)}, f32[8,40,128]{2,1,0:T(8,128)}) custom-call(f32[4,128,1024]{2,1,0:T(8,128)S(1)} %get-tuple-element.31.weight_ref, bf16[4,128,1024]{2,1,0:T(8,128)(2,1)S(1)} %get-tuple-element.32.ds_own_ref, ...), custom_call_target="tpu_custom_call" | custom-call | flops 671088640 | bytes 2097152 | tf_op jit(solution)/shard_map/pallas_call | solution.py:247
  13.4 6.4 %all-to-all-start = ((f32[8,40,128]{2,1,0:T(8,128)}), f32[8,40,128]{2,1,0:T(8,128)S(1)}, u32[]{:S(2)}, u32[]{:S(2)}) async-start(f32[8,40,128]{2,1,0:T(8,128)} %get-tuple-element.37), calls=%async_computation | async-start | bytes 327680 | tf_op jit(solution)/shard_map/all_to_all | solution.py:281
  19.8 1.3 %collective-permute-start.2 = (bf16[2,128,512]{2,1,0:T(8,128)(2,1)S(1)}, bf16[2,128,512]{2,1,0:T(8,128)(2,1)S(1)}, u32[]{:S(2)}, u32[]{:S(2)}) collective-permute-start(bf16[2,128,512]{2,1,0:T(8,128)(2,1)S(1)} %get-tuple-element.38), channel_id=1, source_target_pairs={{32,0},{64,32},{96,64},{128,96},{160,128},{192,160},{224,192},{256... | collective-permute-start | bytes 786440 | tf_op jit(solution)/shard_map/ppermute | solution.py:324
  21.1 8.5 %all-to-all-done = f32[8,40,128]{2,1,0:T(8,128)S(1)} async-done(((f32[8,40,128]{2,1,0:T(8,128)}), f32[8,40,128]{2,1,0:T(8,128)S(1)}, u32[]{:S(2)}, u32[]{:S(2)}) %all-to-all-start) | async-done | bytes 163872 | tf_op jit(solution)/shard_map/all_to_all | solution.py:281
  29.6 9.4 %all_to_all.15 = f32[8,40,128]{2,1,0:T(8,128)S(1)} all-to-all(f32[8,40,128]{2,1,0:T(8,128)S(1)} %broadcast_in_dim.22), channel_id=1, replica_groups={{0,1,2,3,32,33,34,35},{4,5,6,7,36,37,38,39},{8,9,10,11,40,41,42,43},{12..., dimensions={0} | all-to-all | bytes 327680 | tf_op jit(solution)/shard_map/all_to_all | solution.py:281
  39.1 0.0 collective-permute-done.2.returned_ref
  39.1 20.2 %all_to_all.16.parts_ref = f32[8,40,128]{2,1,0:T(8,128)S(1)} all-to-all(f32[8,40,128]{2,1,0:T(8,128)S(1)} %broadcast_in_dim.23), channel_id=1, replica_groups={{0,4,8,12,16,20,24,28},{1,5,9,13,17,21,25,29},{2,6,10,14,18,22,26,30},{..., dimensions={0} | all-to-all | bytes 327680 | tf_op jit(solution)/shard_map/all_to_all | solution.py:281
  59.3 0.7 %shard_map.96 = (f32[40,128]{1,0:T(8,128)}, bf16[128,512]{1,0:T(8,128)(2,1)}, bf16[128,512]{1,0:T(8,128)(2,1)}) custom-call(f32[8,40,128]{2,1,0:T(8,128)S(1)} %all_to_all.16.parts_ref, f32[128,512]{1,0:T(8,128)S(1)} %get-tuple-element.40.key_kept_ref, f32[128,512]{1,0:T(8,128)S(1)} %get-tuple-element.41.value_kept_ref, ...), custom_call_target="tpu_custom_call" | custom-call | tf_op jit(solution)/shard_map/pallas_call | solution.py:302
  (4 shorter events, 0.1 us)
Async XLA Ops:
  0.6 8.4 %collective-permute-start = (bf16[128,512]{1,0:T(8,128)(2,1)}, bf16[128,512]{1,0:T(8,128)(2,1)S(1)}, u32[]{:S(2)}, u32[]{:S(2)}) collective-permute-start(bf16[128,512]{1,0:T(8,128)(2,1)} %bitcast.14), channel_id=1, source_target_pairs={{0,32},{32,64},{64,96},{96,128},{128,160},{160,192},{192,224},{224... | collective-permute-start | bytes 393224 | tf_op jit(solution)/shard_map/ppermute | solution.py:314
  2.4 8.7 %collective-permute-start.1 = (bf16[128,512]{1,0:T(8,128)(2,1)}, bf16[128,512]{1,0:T(8,128)(2,1)S(1)}, u32[]{:S(2)}, u32[]{:S(2)}) collective-permute-start(bf16[128,512]{1,0:T(8,128)(2,1)} %bitcast.16), channel_id=1, source_target_pairs={{0,32},{32,64},{64,96},{96,128},{128,160},{160,192},{192,224},{224... | collective-permute-start | bytes 393224 | tf_op jit(solution)/shard_map/ppermute | solution.py:315
  13.4 16.1 %all-to-all-start = ((f32[8,40,128]{2,1,0:T(8,128)}), f32[8,40,128]{2,1,0:T(8,128)S(1)}, u32[]{:S(2)}, u32[]{:S(2)}) async-start(f32[8,40,128]{2,1,0:T(8,128)} %get-tuple-element.37), calls=%async_computation | async-start | bytes 327680 | tf_op jit(solution)/shard_map/all_to_all | solution.py:281
  19.8 19.3 %collective-permute-start.2 = (bf16[2,128,512]{2,1,0:T(8,128)(2,1)S(1)}, bf16[2,128,512]{2,1,0:T(8,128)(2,1)S(1)}, u32[]{:S(2)}, u32[]{:S(2)}) collective-permute-start(bf16[2,128,512]{2,1,0:T(8,128)(2,1)S(1)} %get-tuple-element.38), channel_id=1, source_target_pairs={{32,0},{64,32},{96,64},{128,96},{160,128},{192,160},{224,192},{256... | collective-permute-start | bytes 786440 | tf_op jit(solution)/shard_map/ppermute | solution.py:324

commit v5 on v4

--- a/solution.py
+++ b/solution.py
@@ -103,12 +103,10 @@
     def scores_of(group):
         return dot(k_before_ref[:, group * HD : (group + 1) * HD], qs_ref[group], NT)
 
-    ahead = scores_of(0)
+    ahead = [scores_of(group) for group in range(shared)]
     for group in range(shared):
         mine = slice(group * HD, (group + 1) * HD)
-        scores_all = ahead
-        if group + 1 < shared:
-            ahead = scores_of(group + 1)
+        scores_all = ahead[group]
         for at in heads():
             peak_own = stat_ref[group, 0:1, at]
             scores = scores_all[:, at] * SCALE2 + mask
@@ -132,7 +130,7 @@
 def score_kernel(
     weight_ref, ds_own_ref, qs_ref, dos_ref, stat_ref, keys_ref, k_before_ref, v_before_ref, value_back_ref, value_sums_ref,
     dq_ref, kept_ref, back_ref, copies_ref,
-    ds_ref, dq_buf, sums_ref, sems,
+    ds_ref, dq_buf, sums_ref, stack_ref, sems,
 ):
     shared = weight_ref.shape[0]
     base = shared * GROUP
@@ -143,13 +141,11 @@
     def grads_of(group):
         return dot(v_before_ref[:, group * HD : (group + 1) * HD], dos_ref[group], NT)
 
-    ahead = grads_of(0)
+    ahead = [grads_of(group) for group in range(shared)]
     for group in range(shared):
         mine = slice(group * HD, (group + 1) * HD)
         keys = jnp.concatenate([k_before_ref[:, mine], keys_ref[:, mine]], axis=0)
-        grads_all = ahead
-        if group + 1 < shared:
-            ahead = grads_of(group + 1)
+        grads_all = ahead[group]
         ds_ref[group, ROWS:, :] = ds_own_ref[group]
         for at in heads():
             slope = weight_ref[group, :, at] * (grads_all[:, at] - stat_ref[group, 2:3, at])
@@ -171,8 +167,9 @@
         kept_ref[:, mine] = key_part[ROWS:]
         sums_ref[base + group : base + group + 1, :] = jnp.sum(key_part, axis=0, keepdims=True)
     for n in range(copies_ref.shape[0]):
-        copies.append(pltpu.make_async_copy(sums_ref, copies_ref.at[n], sems.at[shared + n]))
-        copies[-1].start()
+        stack_ref[n] = sums_ref[...]
+    copies.append(pltpu.make_async_copy(stack_ref, copies_ref, sems.at[shared]))
+    copies[-1].start()
     for copy in copies:
         copy.wait()
 
@@ -258,7 +255,8 @@
             pltpu.VMEM((shared, 2 * ROWS, GROUP * ROWS), jnp.bfloat16),
             pltpu.VMEM((shared, ROWS, GROUP * HD), jnp.bfloat16),
             pltpu.VMEM((rows, HD), jnp.float32),
-            pltpu.SemaphoreType.DMA((shared + peers,)),
+            pltpu.VMEM((peers, rows, HD), jnp.float32),
+            pltpu.SemaphoreType.DMA((shared + 1,)),
         ],
         compiler_params=pltpu.CompilerParams(vmem_limit_bytes=24 * 1024 * 1024),
         cost_estimate=pl.CostEstimate(
@@ -319,14 +317,14 @@
     )
     weights, ds_own, value_kept, value_back, value_sums = weight_part(terms, keys_before)
     query_grad, key_kept, back, copies = score_part(
-        terms, weights, ds_own, keys_before, values_before, value_back, value_sums, ways // 2
+        terms, weights, ds_own, keys_before, values_before, value_back, value_sums, lax.axis_size("dp") // 4
     )
     returned = lax.ppermute(back, "seq", [(i + 1, i) for i in range(ways - 1)])
     places = lax.axis_size("dp")
-    sums = jnp.sum(exchange(copies, bits(2 * places, ways * places)), axis=0)
+    sums = jnp.sum(exchange(copies, bits(4, places)), axis=0)
     sums = jnp.sum(group_parts(sums, [places] + bits(1, 4)), axis=0)
     sums, returned = lax.optimization_barrier((sums, returned))
-    parts = group_parts(sums, bits(4, places))
+    parts = group_parts(sums, bits(2 * places, ways * places))
     bias_grad, key_grad, value_grad = closing(parts, key_kept, value_kept, returned)
     return (query_grad[None], key_grad[None], value_grad[None], bias_grad.reshape(-1))
 

time: 60.3 us -> 60.2 us (level)
  blocking collectives: 29.6 us -> 25.5 us
  starting transfers between devices: 13.2 us -> 17.1 us
    all_to_all x2, blocking collectives: 29.6 us -> 25.5 us  [exchange(): lax.all_to_all(copies, ('seq', 'dp'), split_axis=0, concat_axis=0, tiled=...]
    all_to_all x1, starting transfers between devices: 6.37 us -> 10.3 us  [exchange(): lax.all_to_all(copies, ('seq', 'dp'), split_axis=0, concat_axis=0, tiled=...]
where the time goes in v5:
time: 60.2 us; the launch traced here: 59.8 us
  blocking collectives  25.5 us (42%)
  starting transfers between devices  17.1 us (28%)
  waiting for transfers between devices  8.66 us (14%)
  Pallas kernels  7.78 us (13%)
  between operations  0.73 us (1%)
    all_to_all x2, blocking collectives, exchange(): lax.all_to_all(copies, ('seq', 'dp'), split_axis=0, concat_axis=0, tiled=...  25.5 us
    all_to_all x1, starting transfers between devices, exchange(): lax.all_to_all(copies, ('seq', 'dp'), split_axis=0, concat_axis=0, tiled=...  10.3 us
    all_to_all x1, waiting for transfers between devices, exchange(): lax.all_to_all(copies, ('seq', 'dp'), split_axis=0, concat_axis=0, tiled=...  8.65 us
    ppermute x1, starting transfers between devices, per_device(): values_before = lax.ppermute(value_vectors[0], 'seq', onward)  3.76 us
    pallas_call x1, Pallas kernels, own_part(): pl.pallas_call(own_kernel, in_specs=[SMEM] + [HBM] * 6, out_specs=[VMEM]...  2.9 us
    pallas_call x1, Pallas kernels, score_part(): pl.pallas_call(score_kernel, in_specs=[VMEM] * 10, out_specs=[HBM, VMEM,...  2.23 us
    pallas_call x1, Pallas kernels, weight_part(): pl.pallas_call(weight_kernel, in_specs=[VMEM] * 7, out_specs=[VMEM] * 5,...  1.92 us
    ppermute x1, starting transfers between devices, per_device(): keys_before = lax.ppermute(key_vectors[0], 'seq', onward)  1.75 us
  transfers between devices with their start and end apart: 4, of which 1 were waited for; matrix products, arithmetic and copies ran while one was open for 0% of the time, Pallas kernels for 8%

profile of v5, /device:TPU:2, one launch (start us, length us, event | category | flops | bytes accessed | tf_op | source)
XLA Modules:
  0.0 59.8 jit_solution(4069874262033032670)
XLA Ops:
  0.6 1.7 %collective-permute-start = (bf16[128,512]{1,0:T(8,128)(2,1)}, bf16[128,512]{1,0:T(8,128)(2,1)S(1)}, u32[]{:S(2)}, u32[]{:S(2)}) collective-permute-start(bf16[128,512]{1,0:T(8,128)(2,1)} %bitcast.14), channel_id=1, source_target_pairs={{0,32},{32,64},{64,96},{96,128},{128,160},{160,192},{192,224},{224... | collective-permute-start | bytes 393224 | tf_op jit(solution)/shard_map/ppermute | solution.py:312
  2.4 3.8 %collective-permute-start.1 = (bf16[128,512]{1,0:T(8,128)(2,1)}, bf16[128,512]{1,0:T(8,128)(2,1)S(1)}, u32[]{:S(2)}, u32[]{:S(2)}) collective-permute-start(bf16[128,512]{1,0:T(8,128)(2,1)} %bitcast.16), channel_id=1, source_target_pairs={{0,32},{32,64},{64,96},{96,128},{128,160},{160,192},{192,224},{224... | collective-permute-start | bytes 393224 | tf_op jit(solution)/shard_map/ppermute | solution.py:313
  6.2 2.9 %shard_map.93 = (f32[4,128,1024]{2,1,0:T(8,128)S(1)}, f32[4,128,1024]{2,1,0:T(8,128)S(1)}, bf16[4,1024,128]{2,1,0:T(8,128)(2,1)S(1)}, bf16[4,1024,128]{2,1,0:T(8...) custom-call(s32[1]{0:T(128)} %bitcast.me_ref, ...), custom_call_target="tpu_custom_call" | custom-call | flops 536870912 | bytes 4194304 | tf_op jit(solution)/shard_map/pallas_call | solution.py:182
  9.1 0.0 collective-permute-done.k_before_ref
  9.1 1.9 %shard_map.94 = (f32[4,128,1024]{2,1,0:T(8,128)S(1)}, bf16[4,128,1024]{2,1,0:T(8,128)(2,1)S(1)}, f32[128,512]{1,0:T(8,128)S(1)}, bf16[128,512]{1,0:T(8,128)(2,1)S(1)}, f32[8,128]{1,0:T(8,128)S(1)}) custom-call(f32[4,128,1024]{2,1,0:T(8,128)S(1)} %get-tuple-element.25.power_ref, f32[4,128,1024]{2,1,0:T(8,128)S(1)} %get-tuple-element.26.slope_ref, ...), custom_call_target="tpu_custom_call" | custom-call | flops 402653184 | bytes 1048576 | tf_op jit(solution)/shard_map/pallas_call | solution.py:219
  11.0 0.0 collective-permute-done.1.v_before_ref
  11.0 2.2 %shard_map.95 = (bf16[128,4096]{1,0:T(8,128)(2,1)}, f32[128,512]{1,0:T(8,128)S(1)}, bf16[2,128,512]{2,1,0:T(8,128)(2,1)S(1)}, f32[8,40,128]{2,1,0:T(8,128)}) custom-call(f32[4,128,1024]{2,1,0:T(8,128)S(1)} %get-tuple-element.31.weight_ref, bf16[4,128,1024]{2,1,0:T(8,128)(2,1)S(1)} %get-tuple-element.32.ds_own_ref, ...), custom_call_target="tpu_custom_call" | custom-call | flops 671088640 | bytes 2097152 | tf_op jit(solution)/shard_map/pallas_call | solution.py:244
  13.2 10.3 %all-to-all-start = ((f32[8,40,128]{2,1,0:T(8,128)}), f32[8,40,128]{2,1,0:T(8,128)S(1)}, u32[]{:S(2)}, u32[]{:S(2)}) async-start(f32[8,40,128]{2,1,0:T(8,128)} %get-tuple-element.37), calls=%async_computation | async-start | bytes 327680 | tf_op jit(solution)/shard_map/all_to_all | solution.py:279
  23.6 1.3 %collective-permute-start.2 = (bf16[2,128,512]{2,1,0:T(8,128)(2,1)S(1)}, bf16[2,128,512]{2,1,0:T(8,128)(2,1)S(1)}, u32[]{:S(2)}, u32[]{:S(2)}) collective-permute-start(bf16[2,128,512]{2,1,0:T(8,128)(2,1)S(1)} %get-tuple-element.38), channel_id=1, source_target_pairs={{32,0},{64,32},{96,64},{128,96},{160,128},{192,160},{224,192},{256... | collective-permute-start | bytes 786440 | tf_op jit(solution)/shard_map/ppermute | solution.py:322
  24.9 8.7 %all-to-all-done = f32[8,40,128]{2,1,0:T(8,128)S(1)} async-done(((f32[8,40,128]{2,1,0:T(8,128)}), f32[8,40,128]{2,1,0:T(8,128)S(1)}, u32[]{:S(2)}, u32[]{:S(2)}) %all-to-all-start) | async-done | bytes 163872 | tf_op jit(solution)/shard_map/all_to_all | solution.py:279
  33.5 9.4 %all_to_all.15 = f32[8,40,128]{2,1,0:T(8,128)S(1)} all-to-all(f32[8,40,128]{2,1,0:T(8,128)S(1)} %broadcast_in_dim.22), channel_id=1, replica_groups={{0,1,2,3,32,33,34,35},{4,5,6,7,36,37,38,39},{8,9,10,11,40,41,42,43},{12..., dimensions={0} | all-to-all | bytes 327680 | tf_op jit(solution)/shard_map/all_to_all | solution.py:279
  43.0 0.0 collective-permute-done.2.returned_ref
  43.0 16.1 %all_to_all.16.parts_ref = f32[8,40,128]{2,1,0:T(8,128)S(1)} all-to-all(f32[8,40,128]{2,1,0:T(8,128)S(1)} %broadcast_in_dim.23), channel_id=1, replica_groups={{0,64,128,192,256,320,384,448},{1,65,129,193,257,321,385,449},{2,66,130..., dimensions={0} | all-to-all | bytes 327680 | tf_op jit(solution)/shard_map/all_to_all | solution.py:279
  59.1 0.7 %shard_map.96 = (f32[40,128]{1,0:T(8,128)}, bf16[128,512]{1,0:T(8,128)(2,1)}, bf16[128,512]{1,0:T(8,128)(2,1)}) custom-call(f32[8,40,128]{2,1,0:T(8,128)S(1)} %all_to_all.16.parts_ref, f32[128,512]{1,0:T(8,128)S(1)} %get-tuple-element.40.key_kept_ref, f32[128,512]{1,0:T(8,128)S(1)} %get-tuple-element.41.value_kept_ref, ...), custom_call_target="tpu_custom_call" | custom-call | tf_op jit(solution)/shard_map/pallas_call | solution.py:300
  (4 shorter events, 0.1 us)
Async XLA Ops:
  0.6 8.4 %collective-permute-start = (bf16[128,512]{1,0:T(8,128)(2,1)}, bf16[128,512]{1,0:T(8,128)(2,1)S(1)}, u32[]{:S(2)}, u32[]{:S(2)}) collective-permute-start(bf16[128,512]{1,0:T(8,128)(2,1)} %bitcast.14), channel_id=1, source_target_pairs={{0,32},{32,64},{64,96},{96,128},{128,160},{160,192},{192,224},{224... | collective-permute-start | bytes 393224 | tf_op jit(solution)/shard_map/ppermute | solution.py:312
  2.4 8.6 %collective-permute-start.1 = (bf16[128,512]{1,0:T(8,128)(2,1)}, bf16[128,512]{1,0:T(8,128)(2,1)S(1)}, u32[]{:S(2)}, u32[]{:S(2)}) collective-permute-start(bf16[128,512]{1,0:T(8,128)(2,1)} %bitcast.16), channel_id=1, source_target_pairs={{0,32},{32,64},{64,96},{96,128},{128,160},{160,192},{192,224},{224... | collective-permute-start | bytes 393224 | tf_op jit(solution)/shard_map/ppermute | solution.py:313
  13.2 20.3 %all-to-all-start = ((f32[8,40,128]{2,1,0:T(8,128)}), f32[8,40,128]{2,1,0:T(8,128)S(1)}, u32[]{:S(2)}, u32[]{:S(2)}) async-start(f32[8,40,128]{2,1,0:T(8,128)} %get-tuple-element.37), calls=%async_computation | async-start | bytes 327680 | tf_op jit(solution)/shard_map/all_to_all | solution.py:279
  23.6 19.4 %collective-permute-start.2 = (bf16[2,128,512]{2,1,0:T(8,128)(2,1)S(1)}, bf16[2,128,512]{2,1,0:T(8,128)(2,1)S(1)}, u32[]{:S(2)}, u32[]{:S(2)}) collective-permute-start(bf16[2,128,512]{2,1,0:T(8,128)(2,1)S(1)} %get-tuple-element.38), channel_id=1, source_target_pairs={{32,0},{64,32},{96,64},{128,96},{160,128},{192,160},{224,192},{256... | collective-permute-start | bytes 786440 | tf_op jit(solution)/shard_map/ppermute | solution.py:322

commit v6 on v5

--- a/solution.py
+++ b/solution.py
@@ -317,14 +317,14 @@
     )
     weights, ds_own, value_kept, value_back, value_sums = weight_part(terms, keys_before)
     query_grad, key_kept, back, copies = score_part(
-        terms, weights, ds_own, keys_before, values_before, value_back, value_sums, lax.axis_size("dp") // 4
+        terms, weights, ds_own, keys_before, values_before, value_back, value_sums, ways // 2
     )
     returned = lax.ppermute(back, "seq", [(i + 1, i) for i in range(ways - 1)])
     places = lax.axis_size("dp")
-    sums = jnp.sum(exchange(copies, bits(4, places)), axis=0)
+    sums = jnp.sum(exchange(copies, bits(2 * places, ways * places)), axis=0)
     sums = jnp.sum(group_parts(sums, [places] + bits(1, 4)), axis=0)
     sums, returned = lax.optimization_barrier((sums, returned))
-    parts = group_parts(sums, bits(2 * places, ways * places))
+    parts = group_parts(sums, bits(4, places))
     bias_grad, key_grad, value_grad = closing(parts, key_kept, value_kept, returned)
     return (query_grad[None], key_grad[None], value_grad[None], bias_grad.reshape(-1))
 

time: 60.2 us -> 60.2 us (level)
  blocking collectives: 25.5 us -> 29.6 us
  starting transfers between devices: 17.1 us -> 13.2 us
    all_to_all x2, blocking collectives: 25.5 us -> 29.6 us  [exchange(): lax.all_to_all(copies, ('seq', 'dp'), split_axis=0, concat_axis=0, tiled=...]
    all_to_all x1, starting transfers between devices: 10.3 us -> 6.37 us  [exchange(): lax.all_to_all(copies, ('seq', 'dp'), split_axis=0, concat_axis=0, tiled=...]
where the time goes in v6:
time: 60.2 us; the launch traced here: 59.8 us
  blocking collectives  29.6 us (49%)
  starting transfers between devices  13.2 us (22%)
  waiting for transfers between devices  8.5 us (14%)
  Pallas kernels  7.78 us (13%)
  between operations  0.73 us (1%)
    all_to_all x2, blocking collectives, exchange(): lax.all_to_all(copies, ('seq', 'dp'), split_axis=0, concat_axis=0, tiled=...  29.6 us
    all_to_all x1, waiting for transfers between devices, exchange(): lax.all_to_all(copies, ('seq', 'dp'), split_axis=0, concat_axis=0, tiled=...  8.49 us
    all_to_all x1, starting transfers between devices, exchange(): lax.all_to_all(copies, ('seq', 'dp'), split_axis=0, concat_axis=0, tiled=...  6.37 us
    ppermute x1, starting transfers between devices, per_device(): values_before = lax.ppermute(value_vectors[0], 'seq', onward)  3.76 us
    pallas_call x1, Pallas kernels, own_part(): pl.pallas_call(own_kernel, in_specs=[SMEM] + [HBM] * 6, out_specs=[VMEM]...  2.9 us
    pallas_call x1, Pallas kernels, score_part(): pl.pallas_call(score_kernel, in_specs=[VMEM] * 10, out_specs=[HBM, VMEM,...  2.23 us
    pallas_call x1, Pallas kernels, weight_part(): pl.pallas_call(weight_kernel, in_specs=[VMEM] * 7, out_specs=[VMEM] * 5,...  1.92 us
    ppermute x1, starting transfers between devices, per_device(): keys_before = lax.ppermute(key_vectors[0], 'seq', onward)  1.75 us
  transfers between devices with their start and end apart: 4, of which 1 were waited for; matrix products, arithmetic and copies ran while one was open for 0% of the time, Pallas kernels for 8%

profile of v6, /device:TPU:2, one launch (start us, length us, event | category | flops | bytes accessed | tf_op | source)
XLA Modules:
  0.0 59.8 jit_solution(3241904360433148908)
XLA Ops:
  0.6 1.7 %collective-permute-start = (bf16[128,512]{1,0:T(8,128)(2,1)}, bf16[128,512]{1,0:T(8,128)(2,1)S(1)}, u32[]{:S(2)}, u32[]{:S(2)}) collective-permute-start(bf16[128,512]{1,0:T(8,128)(2,1)} %bitcast.14), channel_id=1, source_target_pairs={{0,32},{32,64},{64,96},{96,128},{128,160},{160,192},{192,224},{224... | collective-permute-start | bytes 393224 | tf_op jit(solution)/shard_map/ppermute | solution.py:312
  2.4 3.8 %collective-permute-start.1 = (bf16[128,512]{1,0:T(8,128)(2,1)}, bf16[128,512]{1,0:T(8,128)(2,1)S(1)}, u32[]{:S(2)}, u32[]{:S(2)}) collective-permute-start(bf16[128,512]{1,0:T(8,128)(2,1)} %bitcast.16), channel_id=1, source_target_pairs={{0,32},{32,64},{64,96},{96,128},{128,160},{160,192},{192,224},{224... | collective-permute-start | bytes 393224 | tf_op jit(solution)/shard_map/ppermute | solution.py:313
  6.2 2.9 %shard_map.93 = (f32[4,128,1024]{2,1,0:T(8,128)S(1)}, f32[4,128,1024]{2,1,0:T(8,128)S(1)}, bf16[4,1024,128]{2,1,0:T(8,128)(2,1)S(1)}, bf16[4,1024,128]{2,1,0:T(8...) custom-call(s32[1]{0:T(128)} %bitcast.me_ref, ...), custom_call_target="tpu_custom_call" | custom-call | flops 536870912 | bytes 4194304 | tf_op jit(solution)/shard_map/pallas_call | solution.py:182
  9.1 0.0 collective-permute-done.k_before_ref
  9.1 1.9 %shard_map.94 = (f32[4,128,1024]{2,1,0:T(8,128)S(1)}, bf16[4,128,1024]{2,1,0:T(8,128)(2,1)S(1)}, f32[128,512]{1,0:T(8,128)S(1)}, bf16[128,512]{1,0:T(8,128)(2,1)S(1)}, f32[8,128]{1,0:T(8,128)S(1)}) custom-call(f32[4,128,1024]{2,1,0:T(8,128)S(1)} %get-tuple-element.25.power_ref, f32[4,128,1024]{2,1,0:T(8,128)S(1)} %get-tuple-element.26.slope_ref, ...), custom_call_target="tpu_custom_call" | custom-call | flops 402653184 | bytes 1048576 | tf_op jit(solution)/shard_map/pallas_call | solution.py:219
  11.0 0.0 collective-permute-done.1.v_before_ref
  11.0 2.2 %shard_map.95 = (bf16[128,4096]{1,0:T(8,128)(2,1)}, f32[128,512]{1,0:T(8,128)S(1)}, bf16[2,128,512]{2,1,0:T(8,128)(2,1)S(1)}, f32[8,40,128]{2,1,0:T(8,128)}) custom-call(f32[4,128,1024]{2,1,0:T(8,128)S(1)} %get-tuple-element.31.weight_ref, bf16[4,128,1024]{2,1,0:T(8,128)(2,1)S(1)} %get-tuple-element.32.ds_own_ref, ...), custom_call_target="tpu_custom_call" | custom-call | flops 671088640 | bytes 2097152 | tf_op jit(solution)/shard_map/pallas_call | solution.py:244
  13.2 6.4 %all-to-all-start = ((f32[8,40,128]{2,1,0:T(8,128)}), f32[8,40,128]{2,1,0:T(8,128)S(1)}, u32[]{:S(2)}, u32[]{:S(2)}) async-start(f32[8,40,128]{2,1,0:T(8,128)} %get-tuple-element.37), calls=%async_computation | async-start | bytes 327680 | tf_op jit(solution)/shard_map/all_to_all | solution.py:279
  19.6 1.3 %collective-permute-start.2 = (bf16[2,128,512]{2,1,0:T(8,128)(2,1)S(1)}, bf16[2,128,512]{2,1,0:T(8,128)(2,1)S(1)}, u32[]{:S(2)}, u32[]{:S(2)}) collective-permute-start(bf16[2,128,512]{2,1,0:T(8,128)(2,1)S(1)} %get-tuple-element.38), channel_id=1, source_target_pairs={{32,0},{64,32},{96,64},{128,96},{160,128},{192,160},{224,192},{256... | collective-permute-start | bytes 786440 | tf_op jit(solution)/shard_map/ppermute | solution.py:322
  20.9 8.5 %all-to-all-done = f32[8,40,128]{2,1,0:T(8,128)S(1)} async-done(((f32[8,40,128]{2,1,0:T(8,128)}), f32[8,40,128]{2,1,0:T(8,128)S(1)}, u32[]{:S(2)}, u32[]{:S(2)}) %all-to-all-start) | async-done | bytes 163872 | tf_op jit(solution)/shard_map/all_to_all | solution.py:279
  29.4 9.4 %all_to_all.15 = f32[8,40,128]{2,1,0:T(8,128)S(1)} all-to-all(f32[8,40,128]{2,1,0:T(8,128)S(1)} %broadcast_in_dim.22), channel_id=1, replica_groups={{0,1,2,3,32,33,34,35},{4,5,6,7,36,37,38,39},{8,9,10,11,40,41,42,43},{12..., dimensions={0} | all-to-all | bytes 327680 | tf_op jit(solution)/shard_map/all_to_all | solution.py:279
  38.9 0.0 collective-permute-done.2.returned_ref
  38.9 20.2 %all_to_all.16.parts_ref = f32[8,40,128]{2,1,0:T(8,128)S(1)} all-to-all(f32[8,40,128]{2,1,0:T(8,128)S(1)} %broadcast_in_dim.23), channel_id=1, replica_groups={{0,4,8,12,16,20,24,28},{1,5,9,13,17,21,25,29},{2,6,10,14,18,22,26,30},{..., dimensions={0} | all-to-all | bytes 327680 | tf_op jit(solution)/shard_map/all_to_all | solution.py:279
  59.1 0.7 %shard_map.96 = (f32[40,128]{1,0:T(8,128)}, bf16[128,512]{1,0:T(8,128)(2,1)}, bf16[128,512]{1,0:T(8,128)(2,1)}) custom-call(f32[8,40,128]{2,1,0:T(8,128)S(1)} %all_to_all.16.parts_ref, f32[128,512]{1,0:T(8,128)S(1)} %get-tuple-element.40.key_kept_ref, f32[128,512]{1,0:T(8,128)S(1)} %get-tuple-element.41.value_kept_ref, ...), custom_call_target="tpu_custom_call" | custom-call | tf_op jit(solution)/shard_map/pallas_call | solution.py:300
  (4 shorter events, 0.1 us)
Async XLA Ops:
  0.6 8.4 %collective-permute-start = (bf16[128,512]{1,0:T(8,128)(2,1)}, bf16[128,512]{1,0:T(8,128)(2,1)S(1)}, u32[]{:S(2)}, u32[]{:S(2)}) collective-permute-start(bf16[128,512]{1,0:T(8,128)(2,1)} %bitcast.14), channel_id=1, source_target_pairs={{0,32},{32,64},{64,96},{96,128},{128,160},{160,192},{192,224},{224... | collective-permute-start | bytes 393224 | tf_op jit(solution)/shard_map/ppermute | solution.py:312
  2.4 8.6 %collective-permute-start.1 = (bf16[128,512]{1,0:T(8,128)(2,1)}, bf16[128,512]{1,0:T(8,128)(2,1)S(1)}, u32[]{:S(2)}, u32[]{:S(2)}) collective-permute-start(bf16[128,512]{1,0:T(8,128)(2,1)} %bitcast.16), channel_id=1, source_target_pairs={{0,32},{32,64},{64,96},{96,128},{128,160},{160,192},{192,224},{224... | collective-permute-start | bytes 393224 | tf_op jit(solution)/shard_map/ppermute | solution.py:313
  13.2 16.1 %all-to-all-start = ((f32[8,40,128]{2,1,0:T(8,128)}), f32[8,40,128]{2,1,0:T(8,128)S(1)}, u32[]{:S(2)}, u32[]{:S(2)}) async-start(f32[8,40,128]{2,1,0:T(8,128)} %get-tuple-element.37), calls=%async_computation | async-start | bytes 327680 | tf_op jit(solution)/shard_map/all_to_all | solution.py:279
  19.6 19.3 %collective-permute-start.2 = (bf16[2,128,512]{2,1,0:T(8,128)(2,1)S(1)}, bf16[2,128,512]{2,1,0:T(8,128)(2,1)S(1)}, u32[]{:S(2)}, u32[]{:S(2)}) collective-permute-start(bf16[2,128,512]{2,1,0:T(8,128)(2,1)S(1)} %get-tuple-element.38), channel_id=1, source_target_pairs={{32,0},{64,32},{96,64},{128,96},{160,128},{192,160},{224,192},{256... | collective-permute-start | bytes 786440 | tf_op jit(solution)/shard_map/ppermute | solution.py:322
